TPU v7x, 32 devices: a whole 2x2x4 slice. The times are simulated.
32 devices in a mesh: lon: 4 (over y, x), lat: 8 (over z, core).
Axes of the slice: x: 2, y: 2, z: 4, core: 2. Of those that a mesh axis runs over, the one named last changes fastest.
Arguments:
- velocity: float32 [3, 64, 96, 384], P(None, 'lon', 'lat'), may hold values from -6 to 6
- pressure_in: float32 [64, 96, 384], P('lon', 'lat')
- viscosity: float32 [64, 96, 384], P('lon', 'lat'), as said below
- body_force: float32 [3, 64, 96, 384], P(None, 'lon', 'lat'), may hold values from -60 to 60
- colour_order: int32 [8], replicated, may hold values from 0 to 7, each once
Outputs:
- velocity_out: float32 [3, 64, 96, 384], P(None, 'lon', 'lat')
- pressure_out: float32 [64, 96, 384], P('lon', 'lat')
Inputs may be any that keep to these rules, and one draw needn't show every extreme that they name: colour_order names each of the 8 colours once. viscosity lies between 1 and 1000000.
All inputs are finite; a program needn't handle non-finite values.
Results may differ from a plain program's by a relative error of at most 0.0003.
Values sent between devices are 32-bit elements; how exact they have to be, the bound alone decides.
No kernel may reach another device: no remote copies, remote signals or barrier semaphores. Data moves between devices by JAX's collectives and lax.ppermute only.
A program may use at most 320 MiB of HBM per device.

v0:
```python
import math

import jax
import jax.numpy as jnp
from jax import lax
from jax.sharding import PartitionSpec as P

SWEEPS = 2
COLOURS = 8


damping = 0.6
coarse_gain = 0.25
unit_steps = ((1, 0, 0), (0, 1, 0), (0, 0, 1))


def extended_2(block, sides, width, periodic):
    for axis, dim in sides:
        count = lax.axis_size(axis)
        forward = [(i, i + 1) for i in range(count - 1)]
        if periodic:
            forward.append((count - 1, 0))
        backward = [(target, source) for source, target in forward]
        low = lax.ppermute(
            lax.slice_in_dim(block, block.shape[dim] - width, None, axis=dim), axis, forward
        )
        high = lax.ppermute(lax.slice_in_dim(block, 0, width, axis=dim), axis, backward)
        block = jnp.concatenate([low, block, high], axis=dim)
    return block


def stencil_offsets():
    result = []
    for step_x in (-1, 0, 1):
        for step_y in (-1, 0, 1):
            for step_z in (-1, 0, 1):
                reach = abs(step_x) + abs(step_y) + abs(step_z)
                if reach > 0:
                    result.append((step_x, step_y, step_z, 0.5 ** (reach - 1)))
    return result


def slide(values, offset, axis_no):
    if offset == 0:
        return values
    extent = values.shape[axis_no]
    padding = [(0, 0)] * values.ndim
    if offset > 0:
        padding[axis_no] = (0, offset)
        return lax.slice_in_dim(jnp.pad(values, padding), offset, offset + extent, axis=axis_no)
    padding[axis_no] = (-offset, 0)
    return lax.slice_in_dim(jnp.pad(values, padding), 0, extent, axis=axis_no)


def moved(values, step_x, step_y, step_z):
    base = values.ndim - 3
    result = slide(values, step_x, base)
    result = slide(result, step_y, base + 1)
    return slide(result, step_z, base + 2)


def blend(own_value, next_value):
    return 2.0 * own_value * next_value / jnp.maximum(own_value + next_value, 1.0)


def viscous_diagonal(viscous):
    running = jnp.zeros_like(viscous)
    for step_x, step_y, step_z, weight in stencil_offsets():
        running = running + weight * blend(viscous, moved(viscous, step_x, step_y, step_z))
    return running


def residuals(fields, viscous, diagonal, body_force):
    velocity = fields[:3]
    pressure = fields[3]
    applied = diagonal * velocity
    for step_x, step_y, step_z, weight in stencil_offsets():
        coupling = weight * blend(viscous, moved(viscous, step_x, step_y, step_z))
        applied = applied - coupling * moved(velocity, step_x, step_y, step_z)
    gradient = jnp.stack(
        [
            moved(pressure, -unit_step[0], -unit_step[1], -unit_step[2]) - pressure
            for unit_step in unit_steps
        ]
    )
    momentum = body_force - applied - gradient
    continuity = jnp.zeros_like(pressure)
    for axis_no, unit_step in enumerate(unit_steps):
        continuity = continuity - (
            moved(velocity[axis_no], unit_step[0], unit_step[1], unit_step[2]) - velocity[axis_no]
        )
    return (momentum, continuity)


def colour_step(fields, viscous, diagonal, inverse, weight_sum, body_force, chosen):
    momentum, continuity = residuals(fields, viscous, diagonal, body_force)
    scaled = momentum * inverse
    mismatch = -continuity
    for axis_no, unit_step in enumerate(unit_steps):
        mismatch = (
            mismatch
            + moved(scaled[axis_no], unit_step[0], unit_step[1], unit_step[2])
            - scaled[axis_no]
        )
    change = chosen * mismatch / weight_sum
    updates = []
    for axis_no, unit_step in enumerate(unit_steps):
        before = moved(chosen, -unit_step[0], -unit_step[1], -unit_step[2])
        earlier = moved(change, -unit_step[0], -unit_step[1], -unit_step[2])
        updates.append(inverse * ((chosen + before) * momentum[axis_no] + change - earlier))
    velocity = fields[:3] + damping * jnp.stack(updates)
    pressure = fields[3] + damping * change
    return jnp.concatenate([velocity, pressure[None]], axis=0)


def colour_codes(shape):
    lon_parity = jnp.arange(shape[0], dtype=jnp.int32) % 2
    lat_parity = jnp.arange(shape[1], dtype=jnp.int32) % 2
    rad_parity = jnp.arange(shape[2], dtype=jnp.int32) % 2
    return lon_parity[:, None, None] + 2 * lat_parity[None, :, None] + 4 * rad_parity[None, None, :]


def extend(fields, margin):
    beside_all = extended_2(fields, (("lon", 1),), margin, True)
    return extended_2(beside_all, (("lat", 2),), margin, False)


def cycle_kernel(distance, cycle_cells):
    decay_rate = 4.0 / cycle_cells
    screening = 2.0 * math.cosh(decay_rate) - 2.0
    factor = screening / (2.0 * math.sinh(decay_rate) * math.sinh(decay_rate * cycle_cells / 2.0))
    wrapped = jnp.mod(distance, cycle_cells).astype(jnp.float32)
    return factor * jnp.cosh(decay_rate * (cycle_cells / 2.0 - wrapped))


def body(velocity, pressure_in, viscosity, body_force, colour_order):
    groups = 1
    margin = 2 * groups
    lon_cells, lat_cells, rad_cells = viscosity.shape
    lat_total = lax.axis_size("lat") * lat_cells
    lat_global = (
        lax.axis_index("lat") * lat_cells
        - margin
        + jnp.arange(lat_cells + 2 * margin, dtype=jnp.int32)
    )
    inside_lat = ((lat_global >= 0) & (lat_global < lat_total)).astype(jnp.float32)
    inside = jnp.broadcast_to(
        inside_lat[None, :, None], (lon_cells + 2 * margin, lat_cells + 2 * margin, rad_cells)
    )
    constant_fields = jnp.concatenate([body_force, viscosity[None]], axis=0)
    constant_wide = extended_2(constant_fields, (("lon", 1), ("lat", 2)), margin, True) * inside
    force_wide = constant_wide[:3]
    viscous_wide = constant_wide[3]
    diagonal = viscous_diagonal(viscous_wide)
    inverse = jnp.where(inside > 0, 1.0 / jnp.where(diagonal > 0, diagonal, 1.0), 0.0)
    weight_raw = 3.0 * inverse
    for unit_step in unit_steps:
        weight_raw = weight_raw + moved(inverse, unit_step[0], unit_step[1], unit_step[2])
    weight_sum = jnp.where(weight_raw > 0, weight_raw, 1.0)
    parity_code = colour_codes(inside.shape)
    fields = jnp.concatenate([velocity, (pressure_in * viscosity)[None]], axis=0)

    def sweep_block(block_no, current):
        extended = extend(current, margin)
        colour = colour_order[(block_no * groups + 0) % COLOURS]
        chosen = (parity_code == colour).astype(jnp.float32) * inside
        extended = colour_step(
            extended, viscous_wide, diagonal, inverse, weight_sum, force_wide, chosen
        )
        return extended[:, margin : margin + lon_cells, margin : margin + lat_cells, :]

    fields = lax.fori_loop(0, SWEEPS * COLOURS // groups, sweep_block, fields)
    extended = extend(fields, margin)
    momentum, continuity = residuals(extended, viscous_wide, diagonal, force_wide)
    momentum = momentum[:, margin : margin + lon_cells, margin : margin + lat_cells, :]
    lon_coarse = lon_cells // 8
    lat_coarse = lat_cells // 4
    rad_coarse = rad_cells // 4
    cycle_cells = lax.axis_size("lon") * lon_coarse
    own_first = lax.axis_index("lon") * lon_coarse
    summed = momentum.reshape(3, lon_coarse, 8, lat_coarse, 4, rad_coarse, 4).sum(axis=(2, 4, 6))
    viscous_sum = viscosity.reshape(lon_coarse, 8, lat_coarse, 4, rad_coarse, 4).sum(axis=(1, 3, 5))
    coarse = jnp.transpose(summed / viscous_sum[None], (1, 0, 2, 3))
    shard_piece = lax.all_gather(coarse, "lon", axis=0, tiled=True)
    sources = jnp.arange(shard_piece.shape[0], dtype=jnp.int32)
    targets = own_first + jnp.arange(lon_coarse, dtype=jnp.int32)
    kernel_table = cycle_kernel(targets[None, :] - sources[:, None], cycle_cells)
    smooth = jnp.einsum("jcyz,ji->icyz", shard_piece, kernel_table, precision=lax.Precision.HIGHEST)
    smooth = jnp.transpose(smooth, (1, 0, 2, 3))
    spread = jnp.repeat(jnp.repeat(jnp.repeat(smooth, 8, axis=1), 4, axis=2), 4, axis=3)
    velocity_out = fields[:3] + coarse_gain * spread
    pressure_out = fields[3] / viscosity
    return (velocity_out, pressure_out)


def solution(mesh):
    placed = (
        P(None, "lon", "lat", None),
        P("lon", "lat", None),
        P("lon", "lat", None),
        P(None, "lon", "lat", None),
        P(),
    )
    return jax.shard_map(
        body,
        mesh=mesh,
        in_specs=placed,
        out_specs=(P(None, "lon", "lat", None), P("lon", "lat", None)),
        check_vma=False,
    )
```

profile of v0, /device:TPU:9, one launch (start us, length us, event | category | flops | bytes accessed | tf_op | source)
XLA Modules:
  0.0 853.1 jit_solution(2724336147057137415)
XLA Ops:
  29.7 6.7 fusion.140
  37.4 688.8 %while.16 = (s32[]{:T(128)}, f32[4,16,12,384]{3,2,1,0:T(8,128)S(1)}, s32[8]{0:T(128)}, f32[20,16,384]{2,1,0:T(8,128)}, f32[20,16,384]{2,1,0:T(8,128)S(1)}, /*ind...) while((s32[]{:T(128)}, ...), condition=%wide.region_1.2_spmd.clone, body=%wide.region_0.1_spmd.clone.sunk | while | flops 44777472 | bytes 127703776 | solution.py:172
  64.0 10.8 %broadcast_multiply_fusion.4 = (f32[3,20,16,384]{3,2,1,0:T(8,128)S(1)}, f32[3,20,16,384]{3,2,1,0:T(8,128)S(1)}) fusion(f32[20,16,384]{2,1,0:T(8,128)S(1)} %get-tuple-element.668, f32[1,20,16,384]{3,2,1,0:T(8,128)} %get-tuple-element.575, f32[1,20,16,384]{3,2,1,0:T(8,128)} %get-tuple-element.576, f32[1,20,16,384]{3,2,1,0:T(8,128)} %get-tuple-element.577, ...), kind=kLoop, calls=%fused_computation.81.clone.1 | loop fusion | flops 21381120 | bytes 32931840 | tf_op jit(solution)/shard_map/while/body/eval_jaxpr/mul | solution.py:97
  107.2 10.8 %broadcast_multiply_fusion.4 = (f32[3,20,16,384]{3,2,1,0:T(8,128)S(1)}, f32[3,20,16,384]{3,2,1,0:T(8,128)S(1)}) fusion(f32[20,16,384]{2,1,0:T(8,128)S(1)} %get-tuple-element.668, f32[1,20,16,384]{3,2,1,0:T(8,128)} %get-tuple-element.575, f32[1,20,16,384]{3,2,1,0:T(8,128)} %get-tuple-element.576, f32[1,20,16,384]{3,2,1,0:T(8,128)} %get-tuple-element.577, ...), kind=kLoop, calls=%fused_computation.81.clone.1 | loop fusion | flops 21381120 | bytes 32931840 | tf_op jit(solution)/shard_map/while/body/eval_jaxpr/mul | solution.py:97
  150.3 10.8 %broadcast_multiply_fusion.4 = (f32[3,20,16,384]{3,2,1,0:T(8,128)S(1)}, f32[3,20,16,384]{3,2,1,0:T(8,128)S(1)}) fusion(f32[20,16,384]{2,1,0:T(8,128)S(1)} %get-tuple-element.668, f32[1,20,16,384]{3,2,1,0:T(8,128)} %get-tuple-element.575, f32[1,20,16,384]{3,2,1,0:T(8,128)} %get-tuple-element.576, f32[1,20,16,384]{3,2,1,0:T(8,128)} %get-tuple-element.577, ...), kind=kLoop, calls=%fused_computation.81.clone.1 | loop fusion | flops 21381120 | bytes 32931840 | tf_op jit(solution)/shard_map/while/body/eval_jaxpr/mul | solution.py:97
  193.4 10.8 %broadcast_multiply_fusion.4 = (f32[3,20,16,384]{3,2,1,0:T(8,128)S(1)}, f32[3,20,16,384]{3,2,1,0:T(8,128)S(1)}) fusion(f32[20,16,384]{2,1,0:T(8,128)S(1)} %get-tuple-element.668, f32[1,20,16,384]{3,2,1,0:T(8,128)} %get-tuple-element.575, f32[1,20,16,384]{3,2,1,0:T(8,128)} %get-tuple-element.576, f32[1,20,16,384]{3,2,1,0:T(8,128)} %get-tuple-element.577, ...), kind=kLoop, calls=%fused_computation.81.clone.1 | loop fusion | flops 21381120 | bytes 32931840 | tf_op jit(solution)/shard_map/while/body/eval_jaxpr/mul | solution.py:97
  236.6 10.8 %broadcast_multiply_fusion.4 = (f32[3,20,16,384]{3,2,1,0:T(8,128)S(1)}, f32[3,20,16,384]{3,2,1,0:T(8,128)S(1)}) fusion(f32[20,16,384]{2,1,0:T(8,128)S(1)} %get-tuple-element.668, f32[1,20,16,384]{3,2,1,0:T(8,128)} %get-tuple-element.575, f32[1,20,16,384]{3,2,1,0:T(8,128)} %get-tuple-element.576, f32[1,20,16,384]{3,2,1,0:T(8,128)} %get-tuple-element.577, ...), kind=kLoop, calls=%fused_computation.81.clone.1 | loop fusion | flops 21381120 | bytes 32931840 | tf_op jit(solution)/shard_map/while/body/eval_jaxpr/mul | solution.py:97
  279.7 10.8 %broadcast_multiply_fusion.4 = (f32[3,20,16,384]{3,2,1,0:T(8,128)S(1)}, f32[3,20,16,384]{3,2,1,0:T(8,128)S(1)}) fusion(f32[20,16,384]{2,1,0:T(8,128)S(1)} %get-tuple-element.668, f32[1,20,16,384]{3,2,1,0:T(8,128)} %get-tuple-element.575, f32[1,20,16,384]{3,2,1,0:T(8,128)} %get-tuple-element.576, f32[1,20,16,384]{3,2,1,0:T(8,128)} %get-tuple-element.577, ...), kind=kLoop, calls=%fused_computation.81.clone.1 | loop fusion | flops 21381120 | bytes 32931840 | tf_op jit(solution)/shard_map/while/body/eval_jaxpr/mul | solution.py:97
  322.8 10.8 %broadcast_multiply_fusion.4 = (f32[3,20,16,384]{3,2,1,0:T(8,128)S(1)}, f32[3,20,16,384]{3,2,1,0:T(8,128)S(1)}) fusion(f32[20,16,384]{2,1,0:T(8,128)S(1)} %get-tuple-element.668, f32[1,20,16,384]{3,2,1,0:T(8,128)} %get-tuple-element.575, f32[1,20,16,384]{3,2,1,0:T(8,128)} %get-tuple-element.576, f32[1,20,16,384]{3,2,1,0:T(8,128)} %get-tuple-element.577, ...), kind=kLoop, calls=%fused_computation.81.clone.1 | loop fusion | flops 21381120 | bytes 32931840 | tf_op jit(solution)/shard_map/while/body/eval_jaxpr/mul | solution.py:97
  365.9 10.8 %broadcast_multiply_fusion.4 = (f32[3,20,16,384]{3,2,1,0:T(8,128)S(1)}, f32[3,20,16,384]{3,2,1,0:T(8,128)S(1)}) fusion(f32[20,16,384]{2,1,0:T(8,128)S(1)} %get-tuple-element.668, f32[1,20,16,384]{3,2,1,0:T(8,128)} %get-tuple-element.575, f32[1,20,16,384]{3,2,1,0:T(8,128)} %get-tuple-element.576, f32[1,20,16,384]{3,2,1,0:T(8,128)} %get-tuple-element.577, ...), kind=kLoop, calls=%fused_computation.81.clone.1 | loop fusion | flops 21381120 | bytes 32931840 | tf_op jit(solution)/shard_map/while/body/eval_jaxpr/mul | solution.py:97
  409.1 10.8 %broadcast_multiply_fusion.4 = (f32[3,20,16,384]{3,2,1,0:T(8,128)S(1)}, f32[3,20,16,384]{3,2,1,0:T(8,128)S(1)}) fusion(f32[20,16,384]{2,1,0:T(8,128)S(1)} %get-tuple-element.668, f32[1,20,16,384]{3,2,1,0:T(8,128)} %get-tuple-element.575, f32[1,20,16,384]{3,2,1,0:T(8,128)} %get-tuple-element.576, f32[1,20,16,384]{3,2,1,0:T(8,128)} %get-tuple-element.577, ...), kind=kLoop, calls=%fused_computation.81.clone.1 | loop fusion | flops 21381120 | bytes 32931840 | tf_op jit(solution)/shard_map/while/body/eval_jaxpr/mul | solution.py:97
  452.2 10.8 %broadcast_multiply_fusion.4 = (f32[3,20,16,384]{3,2,1,0:T(8,128)S(1)}, f32[3,20,16,384]{3,2,1,0:T(8,128)S(1)}) fusion(f32[20,16,384]{2,1,0:T(8,128)S(1)} %get-tuple-element.668, f32[1,20,16,384]{3,2,1,0:T(8,128)} %get-tuple-element.575, f32[1,20,16,384]{3,2,1,0:T(8,128)} %get-tuple-element.576, f32[1,20,16,384]{3,2,1,0:T(8,128)} %get-tuple-element.577, ...), kind=kLoop, calls=%fused_computation.81.clone.1 | loop fusion | flops 21381120 | bytes 32931840 | tf_op jit(solution)/shard_map/while/body/eval_jaxpr/mul | solution.py:97
  495.3 10.8 %broadcast_multiply_fusion.4 = (f32[3,20,16,384]{3,2,1,0:T(8,128)S(1)}, f32[3,20,16,384]{3,2,1,0:T(8,128)S(1)}) fusion(f32[20,16,384]{2,1,0:T(8,128)S(1)} %get-tuple-element.668, f32[1,20,16,384]{3,2,1,0:T(8,128)} %get-tuple-element.575, f32[1,20,16,384]{3,2,1,0:T(8,128)} %get-tuple-element.576, f32[1,20,16,384]{3,2,1,0:T(8,128)} %get-tuple-element.577, ...), kind=kLoop, calls=%fused_computation.81.clone.1 | loop fusion | flops 21381120 | bytes 32931840 | tf_op jit(solution)/shard_map/while/body/eval_jaxpr/mul | solution.py:97
  538.5 10.8 %broadcast_multiply_fusion.4 = (f32[3,20,16,384]{3,2,1,0:T(8,128)S(1)}, f32[3,20,16,384]{3,2,1,0:T(8,128)S(1)}) fusion(f32[20,16,384]{2,1,0:T(8,128)S(1)} %get-tuple-element.668, f32[1,20,16,384]{3,2,1,0:T(8,128)} %get-tuple-element.575, f32[1,20,16,384]{3,2,1,0:T(8,128)} %get-tuple-element.576, f32[1,20,16,384]{3,2,1,0:T(8,128)} %get-tuple-element.577, ...), kind=kLoop, calls=%fused_computation.81.clone.1 | loop fusion | flops 21381120 | bytes 32931840 | tf_op jit(solution)/shard_map/while/body/eval_jaxpr/mul | solution.py:97
  581.6 10.8 %broadcast_multiply_fusion.4 = (f32[3,20,16,384]{3,2,1,0:T(8,128)S(1)}, f32[3,20,16,384]{3,2,1,0:T(8,128)S(1)}) fusion(f32[20,16,384]{2,1,0:T(8,128)S(1)} %get-tuple-element.668, f32[1,20,16,384]{3,2,1,0:T(8,128)} %get-tuple-element.575, f32[1,20,16,384]{3,2,1,0:T(8,128)} %get-tuple-element.576, f32[1,20,16,384]{3,2,1,0:T(8,128)} %get-tuple-element.577, ...), kind=kLoop, calls=%fused_computation.81.clone.1 | loop fusion | flops 21381120 | bytes 32931840 | tf_op jit(solution)/shard_map/while/body/eval_jaxpr/mul | solution.py:97
  624.7 10.8 %broadcast_multiply_fusion.4 = (f32[3,20,16,384]{3,2,1,0:T(8,128)S(1)}, f32[3,20,16,384]{3,2,1,0:T(8,128)S(1)}) fusion(f32[20,16,384]{2,1,0:T(8,128)S(1)} %get-tuple-element.668, f32[1,20,16,384]{3,2,1,0:T(8,128)} %get-tuple-element.575, f32[1,20,16,384]{3,2,1,0:T(8,128)} %get-tuple-element.576, f32[1,20,16,384]{3,2,1,0:T(8,128)} %get-tuple-element.577, ...), kind=kLoop, calls=%fused_computation.81.clone.1 | loop fusion | flops 21381120 | bytes 32931840 | tf_op jit(solution)/shard_map/while/body/eval_jaxpr/mul | solution.py:97
  667.9 10.8 %broadcast_multiply_fusion.4 = (f32[3,20,16,384]{3,2,1,0:T(8,128)S(1)}, f32[3,20,16,384]{3,2,1,0:T(8,128)S(1)}) fusion(f32[20,16,384]{2,1,0:T(8,128)S(1)} %get-tuple-element.668, f32[1,20,16,384]{3,2,1,0:T(8,128)} %get-tuple-element.575, f32[1,20,16,384]{3,2,1,0:T(8,128)} %get-tuple-element.576, f32[1,20,16,384]{3,2,1,0:T(8,128)} %get-tuple-element.577, ...), kind=kLoop, calls=%fused_computation.81.clone.1 | loop fusion | flops 21381120 | bytes 32931840 | tf_op jit(solution)/shard_map/while/body/eval_jaxpr/mul | solution.py:97
  711.0 10.8 %broadcast_multiply_fusion.4 = (f32[3,20,16,384]{3,2,1,0:T(8,128)S(1)}, f32[3,20,16,384]{3,2,1,0:T(8,128)S(1)}) fusion(f32[20,16,384]{2,1,0:T(8,128)S(1)} %get-tuple-element.668, f32[1,20,16,384]{3,2,1,0:T(8,128)} %get-tuple-element.575, f32[1,20,16,384]{3,2,1,0:T(8,128)} %get-tuple-element.576, f32[1,20,16,384]{3,2,1,0:T(8,128)} %get-tuple-element.577, ...), kind=kLoop, calls=%fused_computation.81.clone.1 | loop fusion | flops 21381120 | bytes 32931840 | tf_op jit(solution)/shard_map/while/body/eval_jaxpr/mul | solution.py:97
  729.6 5.8 reshape.151
  777.2 17.9 %fusion.109 = f32[3,20,16,384]{3,2,1,0:T(8,128)} fusion(f32[3,20,16,384]{3,2,1,0:T(8,128)} %get-tuple-element.425, f32[3,20,16,384]{3,2,1,0:T(8,128)} %copy-done.11, f32[3,20,16,384]{3,2,1,0:T(8,128)} %get-tuple-element.424, f32[3,20,16,384]{3,2,1,0:T(8,128)} %get-tuple-element.422, f32[3,20,16,384]{3,2,1,0:T(8,128)} %copy-done.9, ...), kind=kLoop, calls=%fused_computation.253 | loop fusion | flops 16588800 | bytes 24576000 | tf_op jit(solution)/shard_map/sub | solution.py:79
  805.6 14.3 %reshape.150 = f32[3,2,8,3,4,96,4]{2,1,6,5,4,3,0:T(2,128)} reshape(f32[3,16,12,384]{1,3,2,0:T(8,128)} %copy.53) | data formatting | bytes 1769472 | tf_op jit(solution)/shard_map/reshape | solution.py:181
  819.9 11.6 %reduce_sum.18 = f32[3,2,3,96]{1,3,2,0:T(8,128)S(1)} reduce(f32[3,2,8,3,4,96,4]{2,1,6,5,4,3,0:T(2,128)} %reshape.150, f32[]{:T(128)} %constant.185.clone.1), dimensions={2,4,6}, to_apply=%region_2.3 | reduce | flops 219456 | bytes 891652 | tf_op jit(solution)/shard_map/reduce_sum | solution.py:181
  831.7 6.9 all_gather.3
  840.6 6.9 add.1008
  (813 shorter events, 605.9 us)
Async XLA Ops:
  38.2 10.1 %collective-permute-start = (f32[4,2,12,384]{3,2,1,0:T(8,128)}, f32[4,2,12,384]{3,2,1,0:T(8,128)}, u32[]{:S(2)}, u32[]{:S(2)}) collective-permute-start(f32[4,2,12,384]{3,2,1,0:T(8,128)} %get-tuple-element.570), channel_id=1, source_target_pairs={{0,8},{8,16},{16,24},{24,0},{1,9},{9,17},{17,25},{25,1},{2,10},{10... | collective-permute-start | bytes 442376 | tf_op jit(solution)/shard_map/while/body/eval_jaxpr/ppermute | solution.py:24
  80.1 10.1 %collective-permute-start = (f32[4,2,12,384]{3,2,1,0:T(8,128)}, f32[4,2,12,384]{3,2,1,0:T(8,128)}, u32[]{:S(2)}, u32[]{:S(2)}) collective-permute-start(f32[4,2,12,384]{3,2,1,0:T(8,128)} %get-tuple-element.570), channel_id=1, source_target_pairs={{0,8},{8,16},{16,24},{24,0},{1,9},{9,17},{17,25},{25,1},{2,10},{10... | collective-permute-start | bytes 442376 | tf_op jit(solution)/shard_map/while/body/eval_jaxpr/ppermute | solution.py:24
  123.2 10.1 %collective-permute-start = (f32[4,2,12,384]{3,2,1,0:T(8,128)}, f32[4,2,12,384]{3,2,1,0:T(8,128)}, u32[]{:S(2)}, u32[]{:S(2)}) collective-permute-start(f32[4,2,12,384]{3,2,1,0:T(8,128)} %get-tuple-element.570), channel_id=1, source_target_pairs={{0,8},{8,16},{16,24},{24,0},{1,9},{9,17},{17,25},{25,1},{2,10},{10... | collective-permute-start | bytes 442376 | tf_op jit(solution)/shard_map/while/body/eval_jaxpr/ppermute | solution.py:24
  123.6 10.7 %collective-permute-start.1 = (f32[4,2,12,384]{3,2,1,0:T(8,128)}, f32[4,2,12,384]{3,2,1,0:T(8,128)}, u32[]{:S(2)}, u32[]{:S(2)}) collective-permute-start(f32[4,2,12,384]{3,2,1,0:T(8,128)} %get-tuple-element.571), channel_id=1, source_target_pairs={{8,0},{16,8},{24,16},{0,24},{9,1},{17,9},{25,17},{1,25},{10,2},{18... | collective-permute-start | bytes 442376 | tf_op jit(solution)/shard_map/while/body/eval_jaxpr/ppermute | solution.py:27
  166.3 10.1 %collective-permute-start = (f32[4,2,12,384]{3,2,1,0:T(8,128)}, f32[4,2,12,384]{3,2,1,0:T(8,128)}, u32[]{:S(2)}, u32[]{:S(2)}) collective-permute-start(f32[4,2,12,384]{3,2,1,0:T(8,128)} %get-tuple-element.570), channel_id=1, source_target_pairs={{0,8},{8,16},{16,24},{24,0},{1,9},{9,17},{17,25},{25,1},{2,10},{10... | collective-permute-start | bytes 442376 | tf_op jit(solution)/shard_map/while/body/eval_jaxpr/ppermute | solution.py:24
  166.3 11.1 %collective-permute-start.1 = (f32[4,2,12,384]{3,2,1,0:T(8,128)}, f32[4,2,12,384]{3,2,1,0:T(8,128)}, u32[]{:S(2)}, u32[]{:S(2)}) collective-permute-start(f32[4,2,12,384]{3,2,1,0:T(8,128)} %get-tuple-element.571), channel_id=1, source_target_pairs={{8,0},{16,8},{24,16},{0,24},{9,1},{17,9},{25,17},{1,25},{10,2},{18... | collective-permute-start | bytes 442376 | tf_op jit(solution)/shard_map/while/body/eval_jaxpr/ppermute | solution.py:27
  209.5 10.1 %collective-permute-start = (f32[4,2,12,384]{3,2,1,0:T(8,128)}, f32[4,2,12,384]{3,2,1,0:T(8,128)}, u32[]{:S(2)}, u32[]{:S(2)}) collective-permute-start(f32[4,2,12,384]{3,2,1,0:T(8,128)} %get-tuple-element.570), channel_id=1, source_target_pairs={{0,8},{8,16},{16,24},{24,0},{1,9},{9,17},{17,25},{25,1},{2,10},{10... | collective-permute-start | bytes 442376 | tf_op jit(solution)/shard_map/while/body/eval_jaxpr/ppermute | solution.py:24
  209.5 11.1 %collective-permute-start.1 = (f32[4,2,12,384]{3,2,1,0:T(8,128)}, f32[4,2,12,384]{3,2,1,0:T(8,128)}, u32[]{:S(2)}, u32[]{:S(2)}) collective-permute-start(f32[4,2,12,384]{3,2,1,0:T(8,128)} %get-tuple-element.571), channel_id=1, source_target_pairs={{8,0},{16,8},{24,16},{0,24},{9,1},{17,9},{25,17},{1,25},{10,2},{18... | collective-permute-start | bytes 442376 | tf_op jit(solution)/shard_map/while/body/eval_jaxpr/ppermute | solution.py:27
  252.6 10.1 %collective-permute-start = (f32[4,2,12,384]{3,2,1,0:T(8,128)}, f32[4,2,12,384]{3,2,1,0:T(8,128)}, u32[]{:S(2)}, u32[]{:S(2)}) collective-permute-start(f32[4,2,12,384]{3,2,1,0:T(8,128)} %get-tuple-element.570), channel_id=1, source_target_pairs={{0,8},{8,16},{16,24},{24,0},{1,9},{9,17},{17,25},{25,1},{2,10},{10... | collective-permute-start | bytes 442376 | tf_op jit(solution)/shard_map/while/body/eval_jaxpr/ppermute | solution.py:24
  252.6 11.1 %collective-permute-start.1 = (f32[4,2,12,384]{3,2,1,0:T(8,128)}, f32[4,2,12,384]{3,2,1,0:T(8,128)}, u32[]{:S(2)}, u32[]{:S(2)}) collective-permute-start(f32[4,2,12,384]{3,2,1,0:T(8,128)} %get-tuple-element.571), channel_id=1, source_target_pairs={{8,0},{16,8},{24,16},{0,24},{9,1},{17,9},{25,17},{1,25},{10,2},{18... | collective-permute-start | bytes 442376 | tf_op jit(solution)/shard_map/while/body/eval_jaxpr/ppermute | solution.py:27
  295.7 10.1 %collective-permute-start = (f32[4,2,12,384]{3,2,1,0:T(8,128)}, f32[4,2,12,384]{3,2,1,0:T(8,128)}, u32[]{:S(2)}, u32[]{:S(2)}) collective-permute-start(f32[4,2,12,384]{3,2,1,0:T(8,128)} %get-tuple-element.570), channel_id=1, source_target_pairs={{0,8},{8,16},{16,24},{24,0},{1,9},{9,17},{17,25},{25,1},{2,10},{10... | collective-permute-start | bytes 442376 | tf_op jit(solution)/shard_map/while/body/eval_jaxpr/ppermute | solution.py:24
  295.7 11.1 %collective-permute-start.1 = (f32[4,2,12,384]{3,2,1,0:T(8,128)}, f32[4,2,12,384]{3,2,1,0:T(8,128)}, u32[]{:S(2)}, u32[]{:S(2)}) collective-permute-start(f32[4,2,12,384]{3,2,1,0:T(8,128)} %get-tuple-element.571), channel_id=1, source_target_pairs={{8,0},{16,8},{24,16},{0,24},{9,1},{17,9},{25,17},{1,25},{10,2},{18... | collective-permute-start | bytes 442376 | tf_op jit(solution)/shard_map/while/body/eval_jaxpr/ppermute | solution.py:27
  338.8 10.1 %collective-permute-start = (f32[4,2,12,384]{3,2,1,0:T(8,128)}, f32[4,2,12,384]{3,2,1,0:T(8,128)}, u32[]{:S(2)}, u32[]{:S(2)}) collective-permute-start(f32[4,2,12,384]{3,2,1,0:T(8,128)} %get-tuple-element.570), channel_id=1, source_target_pairs={{0,8},{8,16},{16,24},{24,0},{1,9},{9,17},{17,25},{25,1},{2,10},{10... | collective-permute-start | bytes 442376 | tf_op jit(solution)/shard_map/while/body/eval_jaxpr/ppermute | solution.py:24
  338.8 11.1 %collective-permute-start.1 = (f32[4,2,12,384]{3,2,1,0:T(8,128)}, f32[4,2,12,384]{3,2,1,0:T(8,128)}, u32[]{:S(2)}, u32[]{:S(2)}) collective-permute-start(f32[4,2,12,384]{3,2,1,0:T(8,128)} %get-tuple-element.571), channel_id=1, source_target_pairs={{8,0},{16,8},{24,16},{0,24},{9,1},{17,9},{25,17},{1,25},{10,2},{18... | collective-permute-start | bytes 442376 | tf_op jit(solution)/shard_map/while/body/eval_jaxpr/ppermute | solution.py:27
  382.0 10.1 %collective-permute-start = (f32[4,2,12,384]{3,2,1,0:T(8,128)}, f32[4,2,12,384]{3,2,1,0:T(8,128)}, u32[]{:S(2)}, u32[]{:S(2)}) collective-permute-start(f32[4,2,12,384]{3,2,1,0:T(8,128)} %get-tuple-element.570), channel_id=1, source_target_pairs={{0,8},{8,16},{16,24},{24,0},{1,9},{9,17},{17,25},{25,1},{2,10},{10... | collective-permute-start | bytes 442376 | tf_op jit(solution)/shard_map/while/body/eval_jaxpr/ppermute | solution.py:24
  382.0 11.1 %collective-permute-start.1 = (f32[4,2,12,384]{3,2,1,0:T(8,128)}, f32[4,2,12,384]{3,2,1,0:T(8,128)}, u32[]{:S(2)}, u32[]{:S(2)}) collective-permute-start(f32[4,2,12,384]{3,2,1,0:T(8,128)} %get-tuple-element.571), channel_id=1, source_target_pairs={{8,0},{16,8},{24,16},{0,24},{9,1},{17,9},{25,17},{1,25},{10,2},{18... | collective-permute-start | bytes 442376 | tf_op jit(solution)/shard_map/while/body/eval_jaxpr/ppermute | solution.py:27
  425.1 11.1 %collective-permute-start.1 = (f32[4,2,12,384]{3,2,1,0:T(8,128)}, f32[4,2,12,384]{3,2,1,0:T(8,128)}, u32[]{:S(2)}, u32[]{:S(2)}) collective-permute-start(f32[4,2,12,384]{3,2,1,0:T(8,128)} %get-tuple-element.571), channel_id=1, source_target_pairs={{8,0},{16,8},{24,16},{0,24},{9,1},{17,9},{25,17},{1,25},{10,2},{18... | collective-permute-start | bytes 442376 | tf_op jit(solution)/shard_map/while/body/eval_jaxpr/ppermute | solution.py:27
  468.2 11.1 %collective-permute-start.1 = (f32[4,2,12,384]{3,2,1,0:T(8,128)}, f32[4,2,12,384]{3,2,1,0:T(8,128)}, u32[]{:S(2)}, u32[]{:S(2)}) collective-permute-start(f32[4,2,12,384]{3,2,1,0:T(8,128)} %get-tuple-element.571), channel_id=1, source_target_pairs={{8,0},{16,8},{24,16},{0,24},{9,1},{17,9},{25,17},{1,25},{10,2},{18... | collective-permute-start | bytes 442376 | tf_op jit(solution)/shard_map/while/body/eval_jaxpr/ppermute | solution.py:27
  511.4 11.1 %collective-permute-start.1 = (f32[4,2,12,384]{3,2,1,0:T(8,128)}, f32[4,2,12,384]{3,2,1,0:T(8,128)}, u32[]{:S(2)}, u32[]{:S(2)}) collective-permute-start(f32[4,2,12,384]{3,2,1,0:T(8,128)} %get-tuple-element.571), channel_id=1, source_target_pairs={{8,0},{16,8},{24,16},{0,24},{9,1},{17,9},{25,17},{1,25},{10,2},{18... | collective-permute-start | bytes 442376 | tf_op jit(solution)/shard_map/while/body/eval_jaxpr/ppermute | solution.py:27
  554.5 11.1 %collective-permute-start.1 = (f32[4,2,12,384]{3,2,1,0:T(8,128)}, f32[4,2,12,384]{3,2,1,0:T(8,128)}, u32[]{:S(2)}, u32[]{:S(2)}) collective-permute-start(f32[4,2,12,384]{3,2,1,0:T(8,128)} %get-tuple-element.571), channel_id=1, source_target_pairs={{8,0},{16,8},{24,16},{0,24},{9,1},{17,9},{25,17},{1,25},{10,2},{18... | collective-permute-start | bytes 442376 | tf_op jit(solution)/shard_map/while/body/eval_jaxpr/ppermute | solution.py:27
  597.6 11.1 %collective-permute-start.1 = (f32[4,2,12,384]{3,2,1,0:T(8,128)}, f32[4,2,12,384]{3,2,1,0:T(8,128)}, u32[]{:S(2)}, u32[]{:S(2)}) collective-permute-start(f32[4,2,12,384]{3,2,1,0:T(8,128)} %get-tuple-element.571), channel_id=1, source_target_pairs={{8,0},{16,8},{24,16},{0,24},{9,1},{17,9},{25,17},{1,25},{10,2},{18... | collective-permute-start | bytes 442376 | tf_op jit(solution)/shard_map/while/body/eval_jaxpr/ppermute | solution.py:27
  640.8 11.1 %collective-permute-start.1 = (f32[4,2,12,384]{3,2,1,0:T(8,128)}, f32[4,2,12,384]{3,2,1,0:T(8,128)}, u32[]{:S(2)}, u32[]{:S(2)}) collective-permute-start(f32[4,2,12,384]{3,2,1,0:T(8,128)} %get-tuple-element.571), channel_id=1, source_target_pairs={{8,0},{16,8},{24,16},{0,24},{9,1},{17,9},{25,17},{1,25},{10,2},{18... | collective-permute-start | bytes 442376 | tf_op jit(solution)/shard_map/while/body/eval_jaxpr/ppermute | solution.py:27
  683.9 11.1 %collective-permute-start.1 = (f32[4,2,12,384]{3,2,1,0:T(8,128)}, f32[4,2,12,384]{3,2,1,0:T(8,128)}, u32[]{:S(2)}, u32[]{:S(2)}) collective-permute-start(f32[4,2,12,384]{3,2,1,0:T(8,128)} %get-tuple-element.571), channel_id=1, source_target_pairs={{8,0},{16,8},{24,16},{0,24},{9,1},{17,9},{25,17},{1,25},{10,2},{18... | collective-permute-start | bytes 442376 | tf_op jit(solution)/shard_map/while/body/eval_jaxpr/ppermute | solution.py:27
  726.2 26.5 %collective-permute-start.8 = (f32[4,2,12,384]{3,2,1,0:T(8,128)S(1)}, f32[4,2,12,384]{3,2,1,0:T(8,128)S(1)}, u32[]{:S(2)}, u32[]{:S(2)}) collective-permute-start(f32[4,2,12,384]{3,2,1,0:T(8,128)S(1)} %get-tuple-element.414), channel_id=1, source_target_pairs={{0,8},{8,16},{16,24},{24,0},{1,9},{9,17},{17,25},{25,1},{2,10},{10... | collective-permute-start | bytes 442376 | tf_op jit(solution)/shard_map/ppermute | solution.py:24
  (180 other events, 660.9 us)
where the time goes:
time: 859 us; the launch traced here: 853 us
  other arithmetic  440 us (51%)
  local copies, waits for them, and re-layouts  201 us (23%)
  starting transfers between devices  161 us (19%)
  waiting for transfers between devices  39.1 us (5%)
    mul x16, other arithmetic, colour_step(): scaled = momentum * inverse  173 us
    mul x48, other arithmetic, residuals(): coupling = weight * blend(viscous, moved(viscous, step_x, step_y, step_z))  130 us
    ppermute x36, starting transfers between devices, extended_2(): lax.ppermute(lax.slice_in_dim(block, 0, width, axis=dim), axis, backward)  114 us
    while x256, local copies, waits for them, and re-layouts  50.3 us
    ppermute x36, starting transfers between devices, extended_2(): lax.ppermute(lax.slice_in_dim(block, block.shape[dim] - width, None, axis...  46.7 us
    ppermute x36, waiting for transfers between devices, extended_2(): lax.ppermute(lax.slice_in_dim(block, block.shape[dim] - width, None, axis...  25.9 us
    broadcast_in_dim x16, other arithmetic, colour_step(): return jnp.concatenate([velocity, pressure[None]], axis=0)  21.3 us
    another operation x17, other arithmetic, residuals(): jnp.stack([moved(pressure, -unit_step[0], -unit_step[1], -unit_step[2]) -...  21.3 us
  transfers between devices with their start and end apart: 72, of which 37 were waited for; matrix products, arithmetic and copies ran while one was open for 23% of the time, Pallas kernels for 0%

commit v1 on v0

--- a/solution.py
+++ b/solution.py
@@ -1,16 +1,667 @@
+import functools
 import math
 
 import jax
 import jax.numpy as jnp
 from jax import lax
+from jax.experimental import pallas as pl
+from jax.experimental.pallas import tpu as pltpu
 from jax.sharding import PartitionSpec as P
 
 SWEEPS = 2
 COLOURS = 8
-
-
 damping = 0.6
 coarse_gain = 0.25
+
+HALF = 64
+LANES = 128
+SUBLANES = 16
+Z_MARGIN = 16
+Y_ROWS = 4
+PARITIES = [(py, px, pz) for py in (0, 1) for px in (0, 1) for pz in (0, 1)]
+OFFSETS = [
+    (oy, ox, oz, 0.5 ** (abs(oy) + abs(ox) + abs(oz) - 1))
+    for oy in (-1, 0, 1)
+    for ox in (-1, 0, 1)
+    for oz in (-1, 0, 1)
+    if (oy, ox, oz) != (0, 0, 0)
+]
+STEPS = ((0, 1, 0), (1, 0, 0), (0, 0, 1))
+VMEM = pl.BlockSpec(memory_space=pltpu.VMEM)
+SMEM = pl.BlockSpec(memory_space=pltpu.SMEM)
+
+
+def neighbour(parity, offset):
+    py, px, pz = parity
+    oy, ox, oz = offset[:3]
+    shift = -1 if (py == 0 and oy == -1) else 1 if (py == 1 and oy == 1) else 0
+    x_moved = (px == 0 and ox == -1) or (px == 1 and ox == 1)
+    z_moved = (pz == 0 and oz == -1) or (pz == 1 and oz == 1)
+    return shift, int(x_moved) + 2 * int(z_moved), (py ^ (oy & 1), px ^ (ox & 1), pz ^ (oz & 1))
+
+
+def moved_x(value, px):
+    rows = value.shape[0]
+    number = lax.broadcasted_iota(jnp.int32, value.shape, 0)
+    if px == 0:
+        turned = pltpu.roll(value, rows - 1, 0)
+        edge = number == rows - 1
+    else:
+        turned = pltpu.roll(value, 1, 0)
+        edge = number == 0
+    return jnp.where(edge, pltpu.roll(turned, HALF, 1), turned)
+
+
+def moved_z(value, pz):
+    return pltpu.roll(value, LANES - 1 if pz == 0 else 1, 1)
+
+
+def at(j):
+    return pl.ds(pl.multiple_of(j * SUBLANES, SUBLANES), SUBLANES)
+
+
+def pitch(rows):
+    return rows * SUBLANES + 8
+
+
+def gathered(sums, parity):
+    py, px, pz = parity
+    along_x = sums[1] + moved_z(sums[3], 1 - pz)
+    return sums[0] + moved_x(along_x, 1 - px) + moved_z(sums[2], 1 - pz)
+
+
+def lower_lanes(shape):
+    return lax.broadcasted_iota(jnp.int32, shape, len(shape) - 1) < HALF
+
+
+def assemble_kernel(in_ref, state_ref, state_up_ref, state_down_ref, fixed_ref, fixed_up_ref, fixed_down_ref):
+    rows = in_ref.shape[3]
+
+    def one(j, carry):
+        for f in range(8):
+            own_ref = state_ref if f < 4 else fixed_ref
+            for py in (0, 1):
+                for px in (0, 1):
+                    for t in (0, 1):
+                        a = in_ref[t, f, py, j, px]
+                        b = in_ref[t + 2, f, py, j, px]
+                        low = lower_lanes(a.shape)
+                        even = jnp.where(low, a, pltpu.roll(b, HALF, 1))
+                        odd = jnp.where(low, pltpu.roll(a, HALF, 1), b)
+                        own_ref[f % 4, py, j, px, 0, 8 * t : 8 * t + 8] = even
+                        own_ref[f % 4, py, j, px, 1, 8 * t : 8 * t + 8] = odd
+        return carry
+
+    lax.fori_loop(0, rows, one, 0)
+    for own_ref, up_ref, down_ref in (
+        (state_ref, state_up_ref, state_down_ref), (fixed_ref, fixed_up_ref, fixed_down_ref)
+    ):
+        for f in range(4):
+            for py in (0, 1):
+                down_ref[f, py] = own_ref[f, py, 0:Y_ROWS]
+                up_ref[f, py] = own_ref[f, py, rows - Y_ROWS : rows]
+
+
+def place_rows(source, target_ref, fields, first, count):
+    def one(j, carry):
+        for py, px, pz in PARITIES:
+            for f, g in fields:
+                target_ref[g, py, px, pz, at(first + j)] = source[f, py, j, px, pz]
+        return carry
+
+    lax.fori_loop(0, count, one, 0)
+
+
+def coupling_kernel(own_ref, below_ref, above_ref, *refs):
+    c_refs = refs[:8]
+    d_ref, f_ref, vs_ref, v_ref = refs[8:]
+    rows = own_ref.shape[2]
+    total = rows + 2 * Y_ROWS
+    zero = jnp.zeros(own_ref.shape[-2:], jnp.float32)
+    for py, px, pz in PARITIES:
+        v_ref[0, py, px, pz, at(0)] = zero
+        v_ref[0, py, px, pz, at(total + 1)] = zero
+    for source, first, count in (
+        (below_ref, 0, Y_ROWS), (own_ref, Y_ROWS, rows), (above_ref, Y_ROWS + rows, Y_ROWS)
+    ):
+        place_rows(source, f_ref, ((0, 0), (1, 1), (2, 2)), first, count)
+        place_rows(source, v_ref, ((3, 0),), first + 1, count)
+
+    def couple(j, carry):
+        for parity in PARITIES:
+            py, px, pz = parity
+            mine = v_ref[0, py, px, pz, at(j + 1)]
+            along_z = moved_z(mine, pz)
+            seen = [mine, moved_x(mine, px), along_z, moved_x(along_z, px)]
+            sums = [zero] * 4
+            for n, offset in enumerate(OFFSETS):
+                shift, variant, (ny, nx, nz) = neighbour(parity, offset)
+                other = v_ref[0, ny, nx, nz, at(j + 1 + shift)]
+                value = (2.0 * offset[3]) * seen[variant] * other / jnp.maximum(seen[variant] + other, 1.0)
+                c_refs[4 * py + 2 * px + pz][n, at(j)] = value
+                sums[variant] = sums[variant] + value
+            running = gathered(sums, parity)
+            d_ref[0, py, px, pz, at(j)] = running
+            positive = (running > 0) & (mine > 0)
+            d_ref[1, py, px, pz, at(j)] = jnp.where(positive, 1.0 / jnp.where(positive, running, 1.0), 0.0)
+        return carry
+
+    lax.fori_loop(0, total, couple, 0)
+
+    def weigh(j, carry):
+        for parity in PARITIES:
+            py, px, pz = parity
+            raw = 3.0 * d_ref[1, py, px, pz, at(j)]
+            for step in STEPS:
+                shift, variant, (ny, nx, nz) = neighbour(parity, step)
+                other = d_ref[1, ny, nx, nz, at(j + shift)]
+                if variant == 1:
+                    other = moved_x(other, nx)
+                elif variant == 2:
+                    other = moved_z(other, nz)
+                raw = raw + other
+            inside = (v_ref[0, py, px, pz, at(j + 1)] > 0) & (raw > 0)
+            d_ref[2, py, px, pz, at(j)] = jnp.where(inside, 1.0 / jnp.where(inside, raw, 1.0), 0.0)
+        return carry
+
+    lax.fori_loop(0, total - 1, weigh, 0)
+    for py, px, pz in PARITIES:
+        d_ref[2, py, px, pz, at(total - 1)] = zero
+    for y in range(rows // 2):
+        running = zero
+        for j in (2 * y, 2 * y + 1):
+            for py, px, pz in PARITIES:
+                running = running + own_ref[3, py, j, px, pz]
+        vs_ref[y] = running
+
+
+def partial_momentum(u_ref, c_refs, d_ref, f_ref, parity, components, j):
+    py, px, pz = parity
+    sums = []
+    p_here = u_ref[3, py, px, pz, at(j)]
+    diagonal = d_ref[0, py, px, pz, at(j)]
+    for d in components:
+        first = f_ref[d, py, px, pz, at(j)] + p_here - diagonal * u_ref[d, py, px, pz, at(j)]
+        sums.append([first, None, None, None])
+    for n, offset in enumerate(OFFSETS):
+        shift, variant, (ny, nx, nz) = neighbour(parity, offset)
+        weight = c_refs[4 * py + 2 * px + pz][n, at(j)]
+        for i, d in enumerate(components):
+            value = weight * u_ref[d, ny, nx, nz, at(j + shift)]
+            if offset[:3] == tuple(-s for s in STEPS[d]):
+                value = value - u_ref[3, ny, nx, nz, at(j + shift)]
+            sums[i][variant] = value if sums[i][variant] is None else sums[i][variant] + value
+    return sums
+
+
+def sweep_colour(colour, u_ref, c_refs, d_ref, f_ref, delta_ref, sums_ref, low, high):
+    parity = (colour // 2 % 2, colour % 2, colour // 4)
+    py, px, pz = parity
+    faces = [neighbour(parity, step) for step in STEPS]
+
+    def add_up(j):
+        found = partial_momentum(u_ref, c_refs, d_ref, f_ref, parity, (0, 1, 2), j)
+        for d, (shift, variant, face) in enumerate(faces):
+            found += partial_momentum(u_ref, c_refs, d_ref, f_ref, face, (d,), j + shift)
+        for i, sums in enumerate(found):
+            for v in range(4):
+                sums_ref[i, v] = sums[v]
+
+    def change_row(j):
+        here = [gathered([sums_ref[d, v] for v in range(4)], parity) for d in range(3)]
+        there = [gathered([sums_ref[3 + d, v] for v in range(4)], faces[d][2]) for d in range(3)]
+        inverse = d_ref[1, py, px, pz, at(j)]
+        inverse_there = []
+        total = None
+        for d, (shift, variant, face) in enumerate(faces):
+            inverse_there.append(d_ref[(1,) + face + (at(j + shift),)])
+            term = there[d] * inverse_there[d] + u_ref[(d,) + face + (at(j + shift),)]
+            if variant == 1:
+                term = moved_x(term, face[1])
+            elif variant == 2:
+                term = moved_z(term, face[2])
+            term = term - here[d] * inverse - u_ref[d, py, px, pz, at(j)]
+            total = term if total is None else total + term
+        weight = d_ref[2, py, px, pz, at(j)]
+        change = total * weight
+        for d, (shift, variant, face) in enumerate(faces):
+            delta_ref[d, at(j)] = damping * inverse * (here[d] + change)
+            back = change
+            if variant == 1:
+                back = moved_x(change, px)
+            elif variant == 2:
+                back = moved_z(change, pz)
+            own = there[d]
+            if d == 1 and py == 1:
+                own = jnp.where(weight > 0, own, 0.0)
+            if d == 2 and pz == 1:
+                own = jnp.where(moved_z(weight, pz) > 0, own, 0.0)
+            delta_ref[3 + d, at(j)] = damping * inverse_there[d] * (own - back)
+        delta_ref[6, at(j)] = damping * change
+
+    def work(j, carry):
+        change_row(j - 1)
+        add_up(j)
+        return carry
+
+    def apply(j, carry):
+        for d, (shift, variant, face) in enumerate(faces):
+            u_ref[d, py, px, pz, at(j)] += delta_ref[d, at(j)]
+            u_ref[(d,) + face + (at(j + shift),)] += delta_ref[3 + d, at(j)]
+        u_ref[3, py, px, pz, at(j)] += delta_ref[6, at(j)]
+        return carry
+
+    add_up(low)
+    lax.fori_loop(low + 1, high, work, 0)
+    change_row(high - 1)
+    lax.fori_loop(low, high, apply, 0)
+
+
+def group_bounds(order_ref, group):
+    spoiled = 0
+    for n in range(COLOURS // 2, COLOURS):
+        spoiled = spoiled + order_ref[n] // 2 % 2
+    cut = jnp.where(spoiled == 0, 13, 12)
+    return ((0, 4), (4, 8), (8, cut), (cut, SWEEPS * COLOURS))[group]
+
+
+def run_sweeps(group, order_ref, u_ref, c_refs, d_ref, f_ref, delta_ref, sums_ref, rows):
+    first, end = group_bounds(order_ref, group)
+    last = int(group == 3)
+
+    def one(n, carry):
+        colour = order_ref[n % COLOURS]
+        later = end - 1 - n
+        for k in range(COLOURS):
+            ky = k // 2 % 2
+
+            @pl.when(colour == k)
+            def _(k=k, ky=ky):
+                low = jnp.maximum(Y_ROWS - 1 - later + (1 - ky) * (1 - last), 1 - ky)
+                high = jnp.minimum(Y_ROWS + rows + later + last, 2 * Y_ROWS + rows - 1)
+                sweep_colour(k, u_ref, c_refs, d_ref, f_ref, delta_ref, sums_ref, low, high)
+
+        return carry
+
+    lax.fori_loop(first, end, one, 0)
+
+
+def write_strips(u_ref, up_ref, down_ref, rows):
+    def strip(j, carry):
+        for py, px, pz in PARITIES:
+            for f in range(4):
+                down_ref[f, py, j, px, pz] = u_ref[f, py, px, pz, at(Y_ROWS + j)]
+                up_ref[f, py, j, px, pz] = u_ref[f, py, px, pz, at(rows + j)]
+        return carry
+
+    lax.fori_loop(0, Y_ROWS, strip, 0)
+
+
+def load_margins(below_ref, above_ref, u_ref, rows):
+    fields = tuple((f, f) for f in range(4))
+    place_rows(below_ref, u_ref, fields, 0, Y_ROWS)
+    place_rows(above_ref, u_ref, fields, Y_ROWS + rows, Y_ROWS)
+
+
+def first_kernel(order_ref, own_ref, below_ref, above_ref, *refs):
+    c_refs = refs[:8]
+    d_ref, f_ref, u_ref, up_ref, down_ref, delta_ref, sums_ref = refs[8:]
+    rows = own_ref.shape[2]
+    place_rows(own_ref, u_ref, tuple((f, f) for f in range(4)), Y_ROWS, rows)
+    load_margins(below_ref, above_ref, u_ref, rows)
+    run_sweeps(0, order_ref, u_ref, c_refs, d_ref, f_ref, delta_ref, sums_ref, rows)
+    write_strips(u_ref, up_ref, down_ref, rows)
+
+
+def sweep_kernel(group, order_ref, old_ref, below_ref, above_ref, *refs):
+    c_refs = refs[:8]
+    d_ref, f_ref, u_ref, up_ref, down_ref, delta_ref, sums_ref = refs[8:]
+    rows = u_ref.shape[-2] // SUBLANES - 2 * Y_ROWS
+    load_margins(below_ref, above_ref, u_ref, rows)
+    run_sweeps(group, order_ref, u_ref, c_refs, d_ref, f_ref, delta_ref, sums_ref, rows)
+    write_strips(u_ref, up_ref, down_ref, rows)
+
+
+def pair_sum(value, axis, reach):
+    size = value.shape[axis]
+    number = lax.broadcasted_iota(jnp.int32, value.shape, axis)
+    low = (number // reach) % 2 == 0
+    partner = jnp.where(low, pltpu.roll(value, size - reach, axis), pltpu.roll(value, reach, axis))
+    return value + partner
+
+
+def coarse_sum(value):
+    return pair_sum(pair_sum(pair_sum(value, 1, 1), 0, 1), 0, 2)
+
+
+def cycle_weights(cells):
+    rate = 4.0 / cells
+    screening = 2.0 * math.cosh(rate) - 2.0
+    factor = screening / (2.0 * math.sinh(rate) * math.sinh(rate * cells / 2.0))
+    return [factor * math.cosh(rate * (cells / 2.0 - k)) for k in range(cells)]
+
+
+def final_kernel(order_ref, old_ref, below_ref, above_ref, *refs):
+    c_refs = refs[:8]
+    d_ref, f_ref, vs_ref, u_ref, out_ref, delta_ref, sums_ref, sum_ref = refs[8:]
+    rows = u_ref.shape[-2] // SUBLANES - 2 * Y_ROWS
+    load_margins(below_ref, above_ref, u_ref, rows)
+    run_sweeps(3, order_ref, u_ref, c_refs, d_ref, f_ref, delta_ref, sums_ref, rows)
+    sum_ref[...] = jnp.zeros(sum_ref.shape, jnp.float32)
+
+    def residual(j, carry):
+        y = j // 2
+        for parity in PARITIES:
+            found = partial_momentum(u_ref, c_refs, d_ref, f_ref, parity, (0, 1, 2), Y_ROWS + j)
+            for d in range(3):
+                sum_ref[d, y] = sum_ref[d, y] + gathered(found[d], parity)
+        return carry
+
+    lax.fori_loop(0, rows, residual, 0)
+    sublanes = SUBLANES
+    cells = 2 * sublanes // 4
+    weights = cycle_weights(cells)
+    number = lax.broadcasted_iota(jnp.int32, (SUBLANES, LANES), 0)
+    for y in range(rows // 2):
+        viscous = coarse_sum(vs_ref[y])
+        viscous = jnp.where(viscous > 0, viscous, 1.0)
+        for d in range(3):
+            coarse = coarse_sum(sum_ref[d, y]) / viscous
+            smooth = weights[0] * coarse
+            for k in range(1, cells):
+                turned = pltpu.roll(coarse, sublanes - 4, 0)
+                coarse = jnp.where(number >= sublanes - 4, pltpu.roll(turned, HALF, 1), turned)
+                smooth = smooth + weights[k] * coarse
+            sum_ref[d, y] = coarse_gain * smooth
+
+    def pack(j, carry):
+        for py in (0, 1):
+            for px in (0, 1):
+                for f in range(4):
+                    even = u_ref[f, py, px, 0, at(Y_ROWS + j)]
+                    odd = u_ref[f, py, px, 1, at(Y_ROWS + j)]
+                    if f < 3:
+                        added = sum_ref[f, j // 2]
+                        even = even + added
+                        odd = odd + added
+                    low = lower_lanes(even.shape)
+                    first = jnp.where(low, even, pltpu.roll(odd, HALF, 1))
+                    second = jnp.where(low, pltpu.roll(even, HALF, 1), odd)
+                    for t in (0, 1):
+                        out_ref[t, f, py, j, px] = first[8 * t : 8 * t + 8]
+                        out_ref[t + 2, f, py, j, px] = second[8 * t : 8 * t + 8]
+        return carry
+
+    lax.fori_loop(0, rows, pack, 0)
+
+
+def refresh_pack_kernel(u_ref, left_ref, right_ref):
+    rows = u_ref.shape[-2] // SUBLANES - 2 * Y_ROWS
+    pairs = Z_MARGIN // 2
+    lane = lax.broadcasted_iota(jnp.int32, (SUBLANES, LANES), 1) % HALF
+
+    def one(j, carry):
+        for py in (0, 1):
+            for px in (0, 1):
+                to_left = jnp.zeros((SUBLANES, LANES), jnp.float32)
+                to_right = to_left
+                for f in range(4):
+                    for pz in (0, 1):
+                        slot = 2 * f + pz
+                        value = u_ref[f, py, px, pz, at(Y_ROWS + j)]
+                        mine = (lane >= slot * pairs) & (lane < (slot + 1) * pairs)
+                        to_left = jnp.where(mine, pltpu.roll(value, (slot * pairs - pairs) % LANES, 1), to_left)
+                        to_right = jnp.where(
+                            mine, pltpu.roll(value, (slot * pairs - (HALF - 2 * pairs)) % LANES, 1), to_right
+                        )
+                left_ref[py, j, px] = to_left
+                right_ref[py, j, px] = to_right
+        return carry
+
+    lax.fori_loop(0, rows, one, 0)
+
+
+def refresh_kernel(old_ref, from_left_ref, from_right_ref, u_ref, up_ref, down_ref):
+    rows = u_ref.shape[-2] // SUBLANES - 2 * Y_ROWS
+    pairs = Z_MARGIN // 2
+    lane = lax.broadcasted_iota(jnp.int32, (SUBLANES, LANES), 1) % HALF
+
+    def one(j, carry):
+        for py in (0, 1):
+            for px in (0, 1):
+                low = from_left_ref[py, j, px]
+                high = from_right_ref[py, j, px]
+                for f in range(4):
+                    for pz in (0, 1):
+                        slot = 2 * f + pz
+                        value = u_ref[f, py, px, pz, at(Y_ROWS + j)]
+                        value = jnp.where(lane < pairs, pltpu.roll(low, (-slot * pairs) % LANES, 1), value)
+                        value = jnp.where(
+                            lane >= HALF - pairs,
+                            pltpu.roll(high, (HALF - pairs - slot * pairs) % LANES, 1),
+                            value,
+                        )
+                        u_ref[f, py, px, pz, at(Y_ROWS + j)] = value
+        return carry
+
+    lax.fori_loop(0, rows, one, 0)
+    write_strips(u_ref, up_ref, down_ref, rows)
+
+
+def cut_windows(pieces, out_ref, place, parts):
+    shape = pieces[0].shape
+    tiles = len(pieces)
+    width = tiles * LANES // parts
+    lane = lax.broadcasted_iota(jnp.int32, shape, 1)
+    order = 2 * (lane % HALF) + lane // HALF
+    pieces = [jnp.take_along_axis(piece, order, axis=1) for piece in pieces]
+    pair = lane % HALF
+    for s in range(parts):
+        start = (width * s - Z_MARGIN) // 2
+        first, offset = start // HALF, start % HALF
+        found = jnp.zeros(shape, jnp.float32)
+        if 0 <= first < tiles:
+            found = jnp.where(pair < HALF - offset, pltpu.roll(pieces[first], (-offset) % LANES, 1), found)
+        if 0 <= first + 1 < tiles:
+            found = jnp.where(pair >= HALF - offset, pltpu.roll(pieces[first + 1], (HALF - offset) % LANES, 1), found)
+        if width + 2 * Z_MARGIN < LANES:
+            found = jnp.where(pair < width // 2 + Z_MARGIN, found, 0.0)
+        out_ref[(s,) + place] = found
+
+
+def pack_kernel(velocity_ref, pressure_ref, viscosity_ref, force_ref, out_ref, row_ref):
+    parts, _, _, rows = out_ref.shape[:4]
+    half = out_ref.shape[5]
+    tiles = row_ref.shape[2]
+
+    def one(j, carry):
+        for py in (0, 1):
+            y = 2 * j + py
+            for t in range(tiles):
+                columns = slice(LANES * t, LANES * (t + 1))
+                viscous = viscosity_ref[y, :, columns]
+                row_ref[py, 7, t] = viscous
+                row_ref[py, 3, t] = viscous * pressure_ref[y, :, columns]
+                for d in range(3):
+                    row_ref[py, d, t] = velocity_ref[d, y, :, columns]
+                    row_ref[py, 4 + d, t] = force_ref[d, y, :, columns]
+        for py in (0, 1):
+            for px in (0, 1):
+                for f in range(8):
+                    pieces = [row_ref[py, f, t, pl.ds(px, half, stride=2), :] for t in range(tiles)]
+                    cut_windows(pieces, out_ref, (f, py, j, px), parts)
+        return carry
+
+    lax.fori_loop(0, rows, one, 0)
+
+
+def unpack_kernel(back_ref, viscosity_ref, velocity_ref, pressure_ref, row_ref):
+    parts, fields, _, rows = back_ref.shape[:4]
+    tiles = row_ref.shape[2]
+    width = tiles * LANES // parts
+    shape = back_ref.shape[-2:]
+    lane = lax.broadcasted_iota(jnp.int32, shape, 1)
+    order = HALF * (lane % 2) + lane // 2
+
+    def one(j, carry):
+        for py in (0, 1):
+            for px in (0, 1):
+                for f in range(fields):
+                    pieces = [jnp.zeros(shape, jnp.float32)] * tiles
+                    for s in range(parts):
+                        start = width * s - Z_MARGIN
+                        found = jnp.take_along_axis(back_ref[s, f, py, j, px], order, axis=1)
+                        found = pltpu.roll(found, start % LANES, 1)
+                        for t in range(tiles):
+                            low = max(width * s - LANES * t, 0)
+                            high = min(width * (s + 1) - LANES * t, LANES)
+                            if low < high:
+                                pieces[t] = jnp.where((lane >= low) & (lane < high), found, pieces[t])
+                    for t, piece in enumerate(pieces):
+                        row_ref[py, f, t, pl.ds(px, shape[0], stride=2), :] = piece
+        for py in (0, 1):
+            y = 2 * j + py
+            for t in range(tiles):
+                columns = slice(LANES * t, LANES * (t + 1))
+                for d in range(3):
+                    velocity_ref[d, y, :, columns] = row_ref[py, d, t]
+                pressure_ref[y, :, columns] = row_ref[py, 3, t] / viscosity_ref[y, :, columns]
+        return carry
+
+    lax.fori_loop(0, rows, one, 0)
+
+
+def shaped(*shape):
+    return jax.ShapeDtypeStruct(shape, jnp.float32)
+
+
+def kept(*shape):
+    return pltpu.VMEM(shape, jnp.float32)
+
+
+def hold(value):
+    return pltpu.with_memory_space_constraint(value, pltpu.VMEM)
+
+
+def params(mib):
+    return pltpu.CompilerParams(vmem_limit_bytes=mib * 2**20)
+
+
+def exchange(value_up, value_down, axis, count):
+    below = lax.ppermute(value_up, axis, [(i, i + 1) for i in range(count - 1)])
+    above = lax.ppermute(value_down, axis, [(i + 1, i) for i in range(count - 1)])
+    return below, above
+
+
+def body_windows(velocity, pressure_in, viscosity, body_force, colour_order):
+    lon_cells, lat_cells, rad_cells = viscosity.shape
+    parts = lax.axis_size("lon")
+    lats = lax.axis_size("lat")
+    rows = lat_cells // 2
+    total = rows + 2 * Y_ROWS
+    tile = (SUBLANES, LANES)
+    own = shaped(4, 2, rows, 2, 2, *tile)
+    strip = shaped(4, 2, Y_ROWS, 2, 2, *tile)
+    sent = pl.pallas_call(
+        pack_kernel,
+        out_shape=shaped(parts, 8, 2, rows, 2, lon_cells // 2, LANES),
+        in_specs=[VMEM] * 4,
+        out_specs=VMEM,
+        scratch_shapes=[pltpu.VMEM((2, 8, rad_cells // LANES, lon_cells, LANES), jnp.float32)],
+        compiler_params=params(16),
+    )(
+        velocity.transpose(0, 2, 1, 3), pressure_in.transpose(1, 0, 2),
+        viscosity.transpose(1, 0, 2), body_force.transpose(0, 2, 1, 3),
+    )
+    got = lax.all_to_all(sent, "lon", 0, 0, tiled=True)
+    own_state, state_up, state_down, own_fixed, fixed_up, fixed_down = pl.pallas_call(
+        assemble_kernel,
+        out_shape=(own, strip, strip) * 2,
+        in_specs=[VMEM],
+        out_specs=(VMEM,) * 6,
+        compiler_params=params(16),
+    )(got)
+    fixed_below, fixed_above = exchange(fixed_up, fixed_down, "lat", lats)
+    below, above = exchange(state_up, state_down, "lat", lats)
+    stacked = (2, 2, 2)
+    *couplings, diagonals, force, viscous_sum = pl.pallas_call(
+        coupling_kernel,
+        out_shape=(
+            *[kept(len(OFFSETS), pitch(total), LANES)] * 8,
+            kept(3, *stacked, pitch(total), LANES),
+            kept(3, *stacked, pitch(total), LANES),
+            shaped(rows // 2, *tile),
+        ),
+        in_specs=[VMEM, VMEM, VMEM],
+        out_specs=(VMEM,) * 11,
+        scratch_shapes=[pltpu.VMEM((1,) + stacked + (pitch(total + 2), LANES), jnp.float32)],
+        compiler_params=params(10),
+    )(own_fixed, fixed_below, fixed_above)
+    constants = [hold(array) for array in (*couplings, diagonals, force)]
+    state_type = kept(4, *stacked, pitch(total), LANES)
+    scratch = [
+        pltpu.VMEM((7, pitch(total), LANES), jnp.float32),
+        pltpu.VMEM((6, 4) + tile, jnp.float32),
+    ]
+    state, up, down = pl.pallas_call(
+        first_kernel,
+        out_shape=(state_type, strip, strip),
+        in_specs=[SMEM] + [VMEM] * 13,
+        out_specs=(VMEM, VMEM, VMEM),
+        scratch_shapes=scratch,
+        compiler_params=params(8),
+    )(colour_order, own_state, below, above, *constants)
+    for g in (1, 2):
+        below, above = exchange(up, down, "lat", lats)
+        state, up, down = pl.pallas_call(
+            functools.partial(sweep_kernel, g),
+            out_shape=(state_type, strip, strip),
+            in_specs=[SMEM] + [VMEM] * 13,
+            out_specs=(VMEM, VMEM, VMEM),
+            scratch_shapes=scratch,
+            input_output_aliases={1: 0},
+            compiler_params=params(8),
+        )(colour_order, hold(state), below, above, *constants)
+        if g == 1:
+            packed = shaped(2, rows, 2, *tile)
+            to_left, to_right = pl.pallas_call(
+                refresh_pack_kernel,
+                out_shape=(packed, packed),
+                in_specs=[VMEM],
+                out_specs=(VMEM, VMEM),
+                compiler_params=params(6),
+            )(hold(state))
+            from_left, from_right = exchange(to_right, to_left, "lon", parts)
+            state, up, down = pl.pallas_call(
+                refresh_kernel,
+                out_shape=(state_type, strip, strip),
+                in_specs=[VMEM] * 3,
+                out_specs=(VMEM, VMEM, VMEM),
+                input_output_aliases={0: 0},
+                compiler_params=params(6),
+            )(hold(state), from_left, from_right)
+    below, above = exchange(up, down, "lat", lats)
+    state, packed = pl.pallas_call(
+        final_kernel,
+        out_shape=(state_type, shaped(parts, 4, 2, rows, 2, lon_cells // 2, LANES)),
+        in_specs=[SMEM] + [VMEM] * 14,
+        out_specs=(VMEM, VMEM),
+        scratch_shapes=scratch + [pltpu.VMEM((3, rows // 2) + tile, jnp.float32)],
+        input_output_aliases={1: 0},
+        compiler_params=params(8),
+    )(colour_order, hold(state), below, above, *constants, viscous_sum)
+    back = lax.all_to_all(packed, "lon", 0, 0, tiled=True)
+    velocity_out, pressure_out = pl.pallas_call(
+        unpack_kernel,
+        out_shape=(shaped(3, lat_cells, lon_cells, rad_cells), shaped(lat_cells, lon_cells, rad_cells)),
+        in_specs=[VMEM, VMEM],
+        out_specs=(VMEM, VMEM),
+        scratch_shapes=[pltpu.VMEM((2, 4, rad_cells // LANES, lon_cells, LANES), jnp.float32)],
+        compiler_params=params(16),
+    )(back, viscosity.transpose(1, 0, 2))
+    return velocity_out.transpose(0, 2, 1, 3), pressure_out.transpose(1, 0, 2)
+
+
 unit_steps = ((1, 0, 0), (0, 1, 0), (0, 0, 1))
 
 
@@ -133,7 +784,7 @@
     return factor * jnp.cosh(decay_rate * (cycle_cells / 2.0 - wrapped))
 
 
-def body(velocity, pressure_in, viscosity, body_force, colour_order):
+def body_general(velocity, pressure_in, viscosity, body_force, colour_order):
     groups = 1
     margin = 2 * groups
     lon_cells, lat_cells, rad_cells = viscosity.shape
@@ -193,6 +844,23 @@
     return (velocity_out, pressure_out)
 
 
+def body(velocity, pressure_in, viscosity, body_force, colour_order):
+    lon_cells, lat_cells, rad_cells = viscosity.shape
+    parts = lax.axis_size("lon")
+    fits = (
+        parts == 4
+        and parts * lon_cells == 4 * SUBLANES
+        and lat_cells % 4 == 0
+        and lat_cells >= 2 * Y_ROWS
+        and rad_cells % LANES == 0
+        and rad_cells % (4 * parts) == 0
+        and rad_cells // parts + 2 * Z_MARGIN <= LANES
+        and Z_MARGIN <= rad_cells // parts
+    )
+    chosen = body_windows if fits else body_general
+    return chosen(velocity, pressure_in, viscosity, body_force, colour_order)
+
+
 def solution(mesh):
     placed = (
         P(None, "lon", "lat", None),

time: 859 us -> 242 us (0.28)
  other arithmetic: 440 us -> 0 us
  local copies, waits for them, and re-layouts: 201 us -> 4.26 us
  starting transfers between devices: 161 us -> 30.3 us
  Pallas kernels: 0 us -> 83.1 us
  blocking collectives: 6.95 us -> 60.3 us
  waiting for transfers between devices: 39.1 us -> 61.7 us
    mul x67 -> x0, other arithmetic: 305 us -> none  [the longest x16 173 us: colour_step(): scaled = momentum * inverse]
    ppermute x72 -> x12, starting transfers between devices: 161 us -> 30.3 us  [the longest x6 18.3 us: exchange(): below = lax.ppermute(value_up, axis, [(i, i + 1) for i in range(count - 1)])]
    pallas_call x0 -> x10, Pallas kernels: none -> 83.1 us  [the longest x2 27 us: body_windows(): pl.pallas_call(functools.partial(sweep_kernel, g), out_shape=(state_type,...]
    all_to_all x0 -> x2, blocking collectives: none -> 60.3 us  [the longest x1 38.6 us: body_windows(): got = lax.all_to_all(sent, 'lon', 0, 0, tiled=True)]
    slice x128 -> x0, local copies, waits for them, and re-layouts: 58.1 us -> none  [the longest x49 20.6 us: slide(): return lax.slice_in_dim(jnp.pad(values, padding), 0, extent, axis=axis_no)]
    while x257 -> x0, local copies, waits for them, and re-layouts: 51.7 us -> none
    another operation x33 -> x0, other arithmetic: 40.9 us -> none  [the longest x17 21.3 us: residuals(): jnp.stack([moved(pressure, -unit_step[0], -unit_step[1], -unit_step[2]) -...]
    sub x2 -> x0, other arithmetic: 23.2 us -> none  [the longest x1 17.9 us: residuals(): applied = applied - coupling * moved(velocity, step_x, step_y, step_z)]
  transfers between devices with their start and end apart: 72 -> 12, of which waited for: 37 -> 11; matrix products, arithmetic and copies ran while one was open for 23% -> 0% of each run, Pallas kernels for 0% -> 3%
where the time goes in v1:
time: 242 us; the launch traced here: 240 us
  Pallas kernels  83.1 us (34%)
  waiting for transfers between devices  61.7 us (25%)
  blocking collectives  60.3 us (25%)
  starting transfers between devices  30.3 us (13%)
  local copies, waits for them, and re-layouts  4.26 us (2%)
    all_to_all x1, blocking collectives, body_windows(): got = lax.all_to_all(sent, 'lon', 0, 0, tiled=True)  38.6 us
    ppermute x6, waiting for transfers between devices, exchange(): below = lax.ppermute(value_up, axis, [(i, i + 1) for i in range(count - 1)])  35 us
    pallas_call x2, Pallas kernels, body_windows(): pl.pallas_call(functools.partial(sweep_kernel, g), out_shape=(state_type,...  27 us
    ppermute x6, waiting for transfers between devices, exchange(): lax.ppermute(value_down, axis, [(i + 1, i) for i in range(count - 1)])  26.7 us
    all_to_all x1, blocking collectives, body_windows(): back = lax.all_to_all(packed, 'lon', 0, 0, tiled=True)  21.7 us
    pallas_call x1, Pallas kernels, body_windows(): pl.pallas_call(final_kernel, out_shape=(state_type, shaped(parts, 4, 2, r...  18.7 us
    ppermute x6, starting transfers between devices, exchange(): below = lax.ppermute(value_up, axis, [(i, i + 1) for i in range(count - 1)])  18.3 us
    pallas_call x1, Pallas kernels, body_windows(): pl.pallas_call(first_kernel, out_shape=(state_type, strip, strip), in_spe...  13 us
  transfers between devices with their start and end apart: 12, of which 11 were waited for; matrix products, arithmetic and copies ran while one was open for 0% of the time, Pallas kernels for 3%

profile of v1, /device:TPU:9, one launch (start us, length us, event | category | flops | bytes accessed | tf_op | source)
XLA Modules:
  0.0 240.5 jit_solution(15414538526988331199)
XLA Ops:
  4.9 9.7 %shard_map.68 = f32[4,8,2,6,2,8,128]{6,5,4,3,2,1,0:T(8,128)S(1)} custom-call(f32[3,12,16,384]{3,2,1,0:T(8,128)S(1)} %bitcast.8, f32[12,16,384]{2,1,0:T(8,128)S(1)} %bitcast.10, f32[12,16,384]{2,1,0:T(8,128)S(1)} %bitcast.6, f32[3,12,16,384]{3,2,1,0:T(8,128)S(1)} %bitcast.9), custom_call_target="tpu_custom_call" | custom-call | tf_op jit(solution)/shard_map/pallas_call | solution.py:565
  14.6 38.6 %all_to_all.10.in_ref = f32[4,8,2,6,2,8,128]{6,5,4,3,2,1,0:T(8,128)S(1)} all-to-all(f32[4,8,2,6,2,8,128]{6,5,4,3,2,1,0:T(8,128)S(1)} %shard_map.68), channel_id=1, replica_groups=mesh['lon'=4,'lat'=8] {'lon'}, dimensions={0} | all-to-all | bytes 6291456 | tf_op jit(solution)/shard_map/all_to_all | solution.py:576
  54.7 5.3 %collective-permute-start.2 = (f32[4,2,4,2,2,16,128]{6,5,4,3,2,1,0:T(8,128)S(1)}, f32[4,2,4,2,2,16,128]{6,5,4,3,2,1,0:T(8,128)S(1)}, u32[]{:S(2)}, u32[]{:S(2)}) collective-permute-start(f32[4,2,4,2,2,16,128]{6,5,4,3,2,1,0:T(8,128)S(1)} %get-tuple-element.38), channel_id=1, source_target_pairs={{0,1},{1,2},{2,3},{3,4},{4,5},{5,6},{6,7},{8,9},{9,10},{10,11},{11... | collective-permute-start | bytes 3145736 | tf_op jit(solution)/shard_map/ppermute | solution.py:551
  61.9 3.6 %collective-permute-start = (f32[4,2,4,2,2,16,128]{6,5,4,3,2,1,0:T(8,128)S(1)}, f32[4,2,4,2,2,16,128]{6,5,4,3,2,1,0:T(8,128)S(1)}, u32[]{:S(2)}, u32[]{:S(2)}) collective-permute-start(f32[4,2,4,2,2,16,128]{6,5,4,3,2,1,0:T(8,128)S(1)} %get-tuple-element.35), channel_id=1, source_target_pairs={{0,1},{1,2},{2,3},{3,4},{4,5},{5,6},{6,7},{8,9},{9,10},{10,11},{11... | collective-permute-start | bytes 3145736 | tf_op jit(solution)/shard_map/ppermute | solution.py:551
  67.5 4.2 %collective-permute-done.2.below_ref = f32[4,2,4,2,2,16,128]{6,5,4,3,2,1,0:T(8,128)S(1)} collective-permute-done((f32[4,2,4,2,2,16,128]{6,5,4,3,2,1,0:T(8,128)S(1)}, f32[4,2,4,2,2,16,128]{6,5,4,3,2,1,0:T(8,128)S(1)}, u32[]{:S(2)}, u32[]{:S(2)}) %collective-permute-start.2) | collective-permute-done | bytes 1048608 | tf_op jit(solution)/shard_map/ppermute | solution.py:551
  71.7 4.7 %collective-permute-done.3.above_ref = f32[4,2,4,2,2,16,128]{6,5,4,3,2,1,0:T(8,128)S(1)} collective-permute-done((f32[4,2,4,2,2,16,128]{6,5,4,3,2,1,0:T(8,128)S(1)}, f32[4,2,4,2,2,16,128]{6,5,4,3,2,1,0:T(8,128)S(1)}, u32[]{:S(2)}, u32[]{:S(2)}) %collective-permute-start.3) | collective-permute-done | bytes 1048608 | tf_op jit(solution)/shard_map/ppermute | solution.py:552
  76.4 7.9 %shard_map.70 = (f32[26,232,128]{2,1,0:T(8,128)S(1)}, f32[26,232,128]{2,1,0:T(8,128)S(1)}, f32[26,232,128]{2,1,0:T(8,128)S(1)}, f32[26,232,128]{2,1,0:T(8,128)S(...) custom-call(f32[4,2,6,2,2,16,128]{6,5,4,3,2,1,0:T(8,128)S(1)} %get-t, ...), custom_call_target="tpu_custom_call" | custom-call | tf_op jit(solution)/shard_map/pallas_call | solution.py:587
  84.4 3.0 %collective-permute-done.1.above_ref = f32[4,2,4,2,2,16,128]{6,5,4,3,2,1,0:T(8,128)S(1)} collective-permute-done((f32[4,2,4,2,2,16,128]{6,5,4,3,2,1,0:T(8,128)S(1)}, f32[4,2,4,2,2,16,128]{6,5,4,3,2,1,0:T(8,128)S(1)}, u32[]{:S(2)}, u32[]{:S(2)}) %collective-permute-start.1) | collective-permute-done | bytes 1048608 | tf_op jit(solution)/shard_map/ppermute | solution.py:552
  87.4 13.0 %shard_map.71 = (f32[4,2,2,2,232,128]{5,4,3,2,1,0:T(8,128)S(1)}, f32[4,2,4,2,2,16,128]{6,5,4,3,2,1,0:T(8,128)S(1)}, f32[4,2,4,2,2,16,128]{6,5,4,3,2,1,0:T(8,128)S(1)}) custom-call(s32[8]{0:T(128)S(1)} %copy-done.5, f32[4,2,6,2,2,16,128]{6,5,4,3,2,1,0:T(8,128)S(1)} %get-tuple-element.34.own_ref, ...), custom_call_target="tpu_custom_call" | custom-call | tf_op jit(solution)/shard_map/pallas_call | solution.py:606
  104.7 9.3 %collective-permute-done.4.below_ref = f32[4,2,4,2,2,16,128]{6,5,4,3,2,1,0:T(8,128)S(1)} collective-permute-done((f32[4,2,4,2,2,16,128]{6,5,4,3,2,1,0:T(8,128)S(1)}, f32[4,2,4,2,2,16,128]{6,5,4,3,2,1,0:T(8,128)S(1)}, u32[]{:S(2)}, u32[]{:S(2)}) %collective-permute-start.4) | collective-permute-done | bytes 1048608 | tf_op jit(solution)/shard_map/ppermute | solution.py:551
  114.0 4.4 %collective-permute-done.5.above_ref = f32[4,2,4,2,2,16,128]{6,5,4,3,2,1,0:T(8,128)S(1)} collective-permute-done((f32[4,2,4,2,2,16,128]{6,5,4,3,2,1,0:T(8,128)S(1)}, f32[4,2,4,2,2,16,128]{6,5,4,3,2,1,0:T(8,128)S(1)}, u32[]{:S(2)}, u32[]{:S(2)}) %collective-permute-start.5) | collective-permute-done | bytes 1048608 | tf_op jit(solution)/shard_map/ppermute | solution.py:552
  118.4 14.1 %shard_map.72 = (f32[4,2,2,2,232,128]{5,4,3,2,1,0:T(8,128)S(1)}, f32[4,2,4,2,2,16,128]{6,5,4,3,2,1,0:T(8,128)}, f32[4,2,4,2,2,16,128]{6,5,4,3,2,1,0:T(8,128)}) custom-call(s32[8]{0:T(128)S(1)} %copy-done.5, f32[4,2,2,2,232,128]{5,4,3,2,1,0:T(8,128)S(1)} %get-tuple-element.50.old_ref, ...), custom_call_target="tpu_custom_call", output_to_operand_aliasing={{0}: (1, {})} | custom-call | tf_op jit(solution)/shard_map/pallas_call | solution.py:616
  133.6 2.6 %collective-permute-start.6 = (f32[2,6,2,16,128]{4,3,2,1,0:T(8,128)S(1)}, f32[2,6,2,16,128]{4,3,2,1,0:T(8,128)S(1)}, u32[]{:S(2)}, u32[]{:S(2)}) collective-permute-start(f32[2,6,2,16,128]{4,3,2,1,0:T(8,128)S(1)} %get-tuple-element.54), channel_id=1, source_target_pairs={{0,8},{8,16},{16,24},{1,9},{9,17},{17,25},{2,10},{10,18},{18,26},{... | collective-permute-start | bytes 589832 | tf_op jit(solution)/shard_map/ppermute | solution.py:551
  137.5 2.5 %collective-permute-done.6.from_left_ref = f32[2,6,2,16,128]{4,3,2,1,0:T(8,128)S(1)} collective-permute-done((f32[2,6,2,16,128]{4,3,2,1,0:T(8,128)S(1)}, f32[2,6,2,16,128]{4,3,2,1,0:T(8,128)S(1)}, u32[]{:S(2)}, u32[]{:S(2)}) %collective-permute-start.6) | collective-permute-done | bytes 196640 | tf_op jit(solution)/shard_map/ppermute | solution.py:551
  140.0 5.8 %collective-permute-done.7.from_right_ref = f32[2,6,2,16,128]{4,3,2,1,0:T(8,128)S(1)} collective-permute-done((f32[2,6,2,16,128]{4,3,2,1,0:T(8,128)S(1)}, f32[2,6,2,16,128]{4,3,2,1,0:T(8,128)S(1)}, u32[]{:S(2)}, u32[]{:S(2)}) %collective-permute-start.7) | collective-permute-done | bytes 196640 | tf_op jit(solution)/shard_map/ppermute | solution.py:552
  147.1 2.9 %collective-permute-start.8 = (f32[4,2,4,2,2,16,128]{6,5,4,3,2,1,0:T(8,128)S(1)}, f32[4,2,4,2,2,16,128]{6,5,4,3,2,1,0:T(8,128)S(1)}, u32[]{:S(2)}, u32[]{:S(2)}) collective-permute-start(f32[4,2,4,2,2,16,128]{6,5,4,3,2,1,0:T(8,128)S(1)} %get-tuple-element.57), channel_id=1, source_target_pairs={{0,1},{1,2},{2,3},{3,4},{4,5},{5,6},{6,7},{8,9},{9,10},{10,11},{11... | collective-permute-start | bytes 3145736 | tf_op jit(solution)/shard_map/ppermute | solution.py:551
  152.1 9.6 %collective-permute-done.8.below_ref = f32[4,2,4,2,2,16,128]{6,5,4,3,2,1,0:T(8,128)S(1)} collective-permute-done((f32[4,2,4,2,2,16,128]{6,5,4,3,2,1,0:T(8,128)S(1)}, f32[4,2,4,2,2,16,128]{6,5,4,3,2,1,0:T(8,128)S(1)}, u32[]{:S(2)}, u32[]{:S(2)}) %collective-permute-start.8) | collective-permute-done | bytes 1048608 | tf_op jit(solution)/shard_map/ppermute | solution.py:551
  161.7 4.4 %collective-permute-done.9.above_ref = f32[4,2,4,2,2,16,128]{6,5,4,3,2,1,0:T(8,128)S(1)} collective-permute-done((f32[4,2,4,2,2,16,128]{6,5,4,3,2,1,0:T(8,128)S(1)}, f32[4,2,4,2,2,16,128]{6,5,4,3,2,1,0:T(8,128)S(1)}, u32[]{:S(2)}, u32[]{:S(2)}) %collective-permute-start.9) | collective-permute-done | bytes 1048608 | tf_op jit(solution)/shard_map/ppermute | solution.py:552
  166.1 12.9 %shard_map.75 = (f32[4,2,2,2,232,128]{5,4,3,2,1,0:T(8,128)S(1)}, f32[4,2,4,2,2,16,128]{6,5,4,3,2,1,0:T(8,128)S(1)}, f32[4,2,4,2,2,16,128]{6,5,4,3,2,1,0:T(8,128)S(1)}) custom-call(s32[8]{0:T(128)S(1)} %copy-done.5, f32[4,2,2,2,232,128]{5,4,3,2,1,0:T(8,128)S(1)} %get-tuple-element.56.old_ref, ...), custom_call_target="tpu_custom_call", output_to_operand_aliasing={{0}: (1, {})} | custom-call | tf_op jit(solution)/shard_map/pallas_call | solution.py:616
  183.4 9.3 %collective-permute-done.10.below_ref = f32[4,2,4,2,2,16,128]{6,5,4,3,2,1,0:T(8,128)S(1)} collective-permute-done((f32[4,2,4,2,2,16,128]{6,5,4,3,2,1,0:T(8,128)S(1)}, f32[4,2,4,2,2,16,128]{6,5,4,3,2,1,0:T(8,128)S(1)}, u32[]{:S(2)}, u32[]{:S(2)}) %collective-permute-start.10) | collective-permute-done | bytes 1048608 | tf_op jit(solution)/shard_map/ppermute | solution.py:551
  192.7 4.4 %collective-permute-done.11.above_ref = f32[4,2,4,2,2,16,128]{6,5,4,3,2,1,0:T(8,128)S(1)} collective-permute-done((f32[4,2,4,2,2,16,128]{6,5,4,3,2,1,0:T(8,128)S(1)}, f32[4,2,4,2,2,16,128]{6,5,4,3,2,1,0:T(8,128)S(1)}, u32[]{:S(2)}, u32[]{:S(2)}) %collective-permute-start.11) | collective-permute-done | bytes 1048608 | tf_op jit(solution)/shard_map/ppermute | solution.py:552
  197.1 18.7 %shard_map.76 = (f32[4,2,2,2,232,128]{5,4,3,2,1,0:T(8,128)S(1)}, f32[4,4,2,6,2,8,128]{6,5,4,3,2,1,0:T(8,128)S(1)}) custom-call(s32[8]{0:T(128)S(1)} %copy-done.5, f32[4,2,2,2,232,128]{5,4,3,2,1,0:T(8,128)S(1)} %get-tuple-element.59.old_ref, f32[4,2,4,2,2,16,128]{6,5,4,3,2,1,0:T(8,128)S(1)} %collective-permute-done.10.below_ref, ...), custom_call_target="tpu_custom_call", output_to_operand_aliasing={{0}: (1, {})} | custom-call | tf_op jit(solution)/shard_map/pallas_call | solution.py:644
  215.7 21.7 %all_to_all.11.back_ref = f32[4,4,2,6,2,8,128]{6,5,4,3,2,1,0:T(8,128)S(1)} all-to-all(f32[4,4,2,6,2,8,128]{6,5,4,3,2,1,0:T(8,128)S(1)} %get-tuple-element.63), channel_id=1, replica_groups=mesh['lon'=4,'lat'=8] {'lon'}, dimensions={0} | all-to-all | bytes 3145728 | tf_op jit(solution)/shard_map/all_to_all | solution.py:653
  237.5 3.0 %shard_map.77 = (f32[3,12,16,384]{3,2,1,0:T(8,128)}, f32[12,16,384]{2,1,0:T(8,128)}) custom-call(f32[4,4,2,6,2,8,128]{6,5,4,3,2,1,0:T(8,128)S(1)} %all_to_all.11.back_ref, f32[12,16,384]{2,1,0:T(8,128)S(1)} %bitcast.7), custom_call_target="tpu_custom_call" | custom-call | tf_op jit(solution)/shard_map/pallas_call | solution.py:654
  (24 shorter events, 24.0 us)
Async XLA Ops:
  0.6 1.0 copy-start
  1.6 1.2 copy-start.2
  2.8 1.2 copy-start.3
  3.9 1.0 copy-start.4
  53.2 34.1 %copy-start.5 = (s32[8]{0:T(128)S(1)}, s32[8]{0:T(128)}, u32[]{:S(2)}) copy-start(s32[8]{0:T(128)} %order_ref.7) | copy-start | bytes 100
  54.7 17.0 %collective-permute-start.2 = (f32[4,2,4,2,2,16,128]{6,5,4,3,2,1,0:T(8,128)S(1)}, f32[4,2,4,2,2,16,128]{6,5,4,3,2,1,0:T(8,128)S(1)}, u32[]{:S(2)}, u32[]{:S(2)}) collective-permute-start(f32[4,2,4,2,2,16,128]{6,5,4,3,2,1,0:T(8,128)S(1)} %get-tuple-element.38), channel_id=1, source_target_pairs={{0,1},{1,2},{2,3},{3,4},{4,5},{5,6},{6,7},{8,9},{9,10},{10,11},{11... | collective-permute-start | bytes 3145736 | tf_op jit(solution)/shard_map/ppermute | solution.py:551
  60.0 16.4 %collective-permute-start.3 = (f32[4,2,4,2,2,16,128]{6,5,4,3,2,1,0:T(8,128)S(1)}, f32[4,2,4,2,2,16,128]{6,5,4,3,2,1,0:T(8,128)S(1)}, u32[]{:S(2)}, u32[]{:S(2)}) collective-permute-start(f32[4,2,4,2,2,16,128]{6,5,4,3,2,1,0:T(8,128)S(1)} %get-tuple-element.39), channel_id=1, source_target_pairs={{1,0},{2,1},{3,2},{4,3},{5,4},{6,5},{7,6},{9,8},{10,9},{11,10},{12... | collective-permute-start | bytes 3145736 | tf_op jit(solution)/shard_map/ppermute | solution.py:552
  61.9 22.4 %collective-permute-start = (f32[4,2,4,2,2,16,128]{6,5,4,3,2,1,0:T(8,128)S(1)}, f32[4,2,4,2,2,16,128]{6,5,4,3,2,1,0:T(8,128)S(1)}, u32[]{:S(2)}, u32[]{:S(2)}) collective-permute-start(f32[4,2,4,2,2,16,128]{6,5,4,3,2,1,0:T(8,128)S(1)} %get-tuple-element.35), channel_id=1, source_target_pairs={{0,1},{1,2},{2,3},{3,4},{4,5},{5,6},{6,7},{8,9},{9,10},{10,11},{11... | collective-permute-start | bytes 3145736 | tf_op jit(solution)/shard_map/ppermute | solution.py:551
  65.6 21.8 %collective-permute-start.1 = (f32[4,2,4,2,2,16,128]{6,5,4,3,2,1,0:T(8,128)S(1)}, f32[4,2,4,2,2,16,128]{6,5,4,3,2,1,0:T(8,128)S(1)}, u32[]{:S(2)}, u32[]{:S(2)}) collective-permute-start(f32[4,2,4,2,2,16,128]{6,5,4,3,2,1,0:T(8,128)S(1)} %get-tuple-element.36), channel_id=1, source_target_pairs={{1,0},{2,1},{3,2},{4,3},{5,4},{6,5},{7,6},{9,8},{10,9},{11,10},{12... | collective-permute-start | bytes 3145736 | tf_op jit(solution)/shard_map/ppermute | solution.py:552
  100.3 13.7 %collective-permute-start.4 = (f32[4,2,4,2,2,16,128]{6,5,4,3,2,1,0:T(8,128)S(1)}, f32[4,2,4,2,2,16,128]{6,5,4,3,2,1,0:T(8,128)S(1)}, u32[]{:S(2)}, u32[]{:S(2)}) collective-permute-start(f32[4,2,4,2,2,16,128]{6,5,4,3,2,1,0:T(8,128)S(1)} %get-tuple-element.51), channel_id=1, source_target_pairs={{0,1},{1,2},{2,3},{3,4},{4,5},{5,6},{6,7},{8,9},{9,10},{10,11},{11... | collective-permute-start | bytes 3145736 | tf_op jit(solution)/shard_map/ppermute | solution.py:551
  102.3 16.1 %collective-permute-start.5 = (f32[4,2,4,2,2,16,128]{6,5,4,3,2,1,0:T(8,128)S(1)}, f32[4,2,4,2,2,16,128]{6,5,4,3,2,1,0:T(8,128)S(1)}, u32[]{:S(2)}, u32[]{:S(2)}) collective-permute-start(f32[4,2,4,2,2,16,128]{6,5,4,3,2,1,0:T(8,128)S(1)} %get-tuple-element.52), channel_id=1, source_target_pairs={{1,0},{2,1},{3,2},{4,3},{5,4},{6,5},{7,6},{9,8},{10,9},{11,10},{12... | collective-permute-start | bytes 3145736 | tf_op jit(solution)/shard_map/ppermute | solution.py:552
  133.6 6.4 %collective-permute-start.6 = (f32[2,6,2,16,128]{4,3,2,1,0:T(8,128)S(1)}, f32[2,6,2,16,128]{4,3,2,1,0:T(8,128)S(1)}, u32[]{:S(2)}, u32[]{:S(2)}) collective-permute-start(f32[2,6,2,16,128]{4,3,2,1,0:T(8,128)S(1)} %get-tuple-element.54), channel_id=1, source_target_pairs={{0,8},{8,16},{16,24},{1,9},{9,17},{17,25},{2,10},{10,18},{18,26},{... | collective-permute-start | bytes 589832 | tf_op jit(solution)/shard_map/ppermute | solution.py:551
  136.2 9.6 %collective-permute-start.7 = (f32[2,6,2,16,128]{4,3,2,1,0:T(8,128)S(1)}, f32[2,6,2,16,128]{4,3,2,1,0:T(8,128)S(1)}, u32[]{:S(2)}, u32[]{:S(2)}) collective-permute-start(f32[2,6,2,16,128]{4,3,2,1,0:T(8,128)S(1)} %get-tuple-element.55), channel_id=1, source_target_pairs={{8,0},{16,8},{24,16},{9,1},{17,9},{25,17},{10,2},{18,10},{26,18},{... | collective-permute-start | bytes 589832 | tf_op jit(solution)/shard_map/ppermute | solution.py:552
  147.1 14.6 %collective-permute-start.8 = (f32[4,2,4,2,2,16,128]{6,5,4,3,2,1,0:T(8,128)S(1)}, f32[4,2,4,2,2,16,128]{6,5,4,3,2,1,0:T(8,128)S(1)}, u32[]{:S(2)}, u32[]{:S(2)}) collective-permute-start(f32[4,2,4,2,2,16,128]{6,5,4,3,2,1,0:T(8,128)S(1)} %get-tuple-element.57), channel_id=1, source_target_pairs={{0,1},{1,2},{2,3},{3,4},{4,5},{5,6},{6,7},{8,9},{9,10},{10,11},{11... | collective-permute-start | bytes 3145736 | tf_op jit(solution)/shard_map/ppermute | solution.py:551
  150.0 16.1 %collective-permute-start.9 = (f32[4,2,4,2,2,16,128]{6,5,4,3,2,1,0:T(8,128)S(1)}, f32[4,2,4,2,2,16,128]{6,5,4,3,2,1,0:T(8,128)S(1)}, u32[]{:S(2)}, u32[]{:S(2)}) collective-permute-start(f32[4,2,4,2,2,16,128]{6,5,4,3,2,1,0:T(8,128)S(1)} %get-tuple-element.58), channel_id=1, source_target_pairs={{1,0},{2,1},{3,2},{4,3},{5,4},{6,5},{7,6},{9,8},{10,9},{11,10},{12... | collective-permute-start | bytes 3145736 | tf_op jit(solution)/shard_map/ppermute | solution.py:552
  179.0 13.7 %collective-permute-start.10 = (f32[4,2,4,2,2,16,128]{6,5,4,3,2,1,0:T(8,128)S(1)}, f32[4,2,4,2,2,16,128]{6,5,4,3,2,1,0:T(8,128)S(1)}, u32[]{:S(2)}, u32[]{:S(2)}) collective-permute-start(f32[4,2,4,2,2,16,128]{6,5,4,3,2,1,0:T(8,128)S(1)} %get-tuple-element.60), channel_id=1, source_target_pairs={{0,1},{1,2},{2,3},{3,4},{4,5},{5,6},{6,7},{8,9},{9,10},{10,11},{11... | collective-permute-start | bytes 3145736 | tf_op jit(solution)/shard_map/ppermute | solution.py:551
  180.9 16.1 %collective-permute-start.11 = (f32[4,2,4,2,2,16,128]{6,5,4,3,2,1,0:T(8,128)S(1)}, f32[4,2,4,2,2,16,128]{6,5,4,3,2,1,0:T(8,128)S(1)}, u32[]{:S(2)}, u32[]{:S(2)}) collective-permute-start(f32[4,2,4,2,2,16,128]{6,5,4,3,2,1,0:T(8,128)S(1)} %get-tuple-element.61), channel_id=1, source_target_pairs={{1,0},{2,1},{3,2},{4,3},{5,4},{6,5},{7,6},{9,8},{10,9},{11,10},{12... | collective-permute-start | bytes 3145736 | tf_op jit(solution)/shard_map/ppermute | solution.py:552
  215.7 21.7 %copy-start.1 = (f32[16,12,384]{2,0,1:T(8,128)S(1)}, f32[16,12,384]{2,0,1:T(8,128)}, u32[]{:S(2)}) copy-start(f32[16,12,384]{2,0,1:T(8,128)} %param.7) | copy-start | bytes 884740

commit v2 on v1

--- a/solution.py
+++ b/solution.py
@@ -13,7 +13,6 @@
 damping = 0.6
 coarse_gain = 0.25
 
-HALF = 64
 LANES = 128
 SUBLANES = 16
 Z_MARGIN = 16
@@ -40,6 +39,14 @@
     return shift, int(x_moved) + 2 * int(z_moved), (py ^ (oy & 1), px ^ (ox & 1), pz ^ (oz & 1))
 
 
+def even_lanes(shape):
+    return lax.broadcasted_iota(jnp.int32, shape, len(shape) - 1) % 2 == 0
+
+
+def swapped(value):
+    return jnp.where(even_lanes(value.shape), pltpu.roll(value, LANES - 1, 1), pltpu.roll(value, 1, 1))
+
+
 def moved_x(value, px):
     rows = value.shape[0]
     number = lax.broadcasted_iota(jnp.int32, value.shape, 0)
@@ -49,11 +56,11 @@
     else:
         turned = pltpu.roll(value, 1, 0)
         edge = number == 0
-    return jnp.where(edge, pltpu.roll(turned, HALF, 1), turned)
+    return jnp.where(edge, swapped(turned), turned)
 
 
 def moved_z(value, pz):
-    return pltpu.roll(value, LANES - 1 if pz == 0 else 1, 1)
+    return pltpu.roll(value, LANES - 2 if pz == 0 else 2, 1)
 
 
 def at(j):
@@ -70,36 +77,28 @@
     return sums[0] + moved_x(along_x, 1 - px) + moved_z(sums[2], 1 - pz)
 
 
-def lower_lanes(shape):
-    return lax.broadcasted_iota(jnp.int32, shape, len(shape) - 1) < HALF
-
-
-def assemble_kernel(in_ref, state_ref, state_up_ref, state_down_ref, fixed_ref, fixed_up_ref, fixed_down_ref):
-    rows = in_ref.shape[3]
+def assemble_kernel(in_ref, own_ref, up_ref, down_ref):
+    fields, rows = own_ref.shape[0], own_ref.shape[2]
 
     def one(j, carry):
-        for f in range(8):
-            own_ref = state_ref if f < 4 else fixed_ref
+        for f in range(fields):
             for py in (0, 1):
                 for px in (0, 1):
                     for t in (0, 1):
                         a = in_ref[t, f, py, j, px]
                         b = in_ref[t + 2, f, py, j, px]
-                        low = lower_lanes(a.shape)
-                        even = jnp.where(low, a, pltpu.roll(b, HALF, 1))
-                        odd = jnp.where(low, pltpu.roll(a, HALF, 1), b)
-                        own_ref[f % 4, py, j, px, 0, 8 * t : 8 * t + 8] = even
-                        own_ref[f % 4, py, j, px, 1, 8 * t : 8 * t + 8] = odd
+                        low = even_lanes(a.shape)
+                        even = jnp.where(low, a, pltpu.roll(b, 1, 1))
+                        odd = jnp.where(low, pltpu.roll(a, LANES - 1, 1), b)
+                        own_ref[f, py, j, px, 0, 8 * t : 8 * t + 8] = even
+                        own_ref[f, py, j, px, 1, 8 * t : 8 * t + 8] = odd
         return carry
 
     lax.fori_loop(0, rows, one, 0)
-    for own_ref, up_ref, down_ref in (
-        (state_ref, state_up_ref, state_down_ref), (fixed_ref, fixed_up_ref, fixed_down_ref)
-    ):
-        for f in range(4):
-            for py in (0, 1):
-                down_ref[f, py] = own_ref[f, py, 0:Y_ROWS]
-                up_ref[f, py] = own_ref[f, py, rows - Y_ROWS : rows]
+    for f in range(fields):
+        for py in (0, 1):
+            down_ref[f, py] = own_ref[f, py, 0:Y_ROWS]
+            up_ref[f, py] = own_ref[f, py, rows - Y_ROWS : rows]
 
 
 def place_rows(source, target_ref, fields, first, count):
@@ -199,17 +198,17 @@
     py, px, pz = parity
     faces = [neighbour(parity, step) for step in STEPS]
 
-    def add_up(j):
+    def add_up(j, slot):
         found = partial_momentum(u_ref, c_refs, d_ref, f_ref, parity, (0, 1, 2), j)
         for d, (shift, variant, face) in enumerate(faces):
             found += partial_momentum(u_ref, c_refs, d_ref, f_ref, face, (d,), j + shift)
         for i, sums in enumerate(found):
             for v in range(4):
-                sums_ref[i, v] = sums[v]
-
-    def change_row(j):
-        here = [gathered([sums_ref[d, v] for v in range(4)], parity) for d in range(3)]
-        there = [gathered([sums_ref[3 + d, v] for v in range(4)], faces[d][2]) for d in range(3)]
+                sums_ref[slot, i, v] = sums[v]
+
+    def change_row(j, slot):
+        here = [gathered([sums_ref[slot, d, v] for v in range(4)], parity) for d in range(3)]
+        there = [gathered([sums_ref[slot, 3 + d, v] for v in range(4)], faces[d][2]) for d in range(3)]
         inverse = d_ref[1, py, px, pz, at(j)]
         inverse_there = []
         total = None
@@ -239,9 +238,11 @@
             delta_ref[3 + d, at(j)] = damping * inverse_there[d] * (own - back)
         delta_ref[6, at(j)] = damping * change
 
-    def work(j, carry):
-        change_row(j - 1)
-        add_up(j)
+    def work(i, carry):
+        for slot in (0, 1):
+            change_row(jnp.clip(low + 2 * i - 2 + slot, low, high - 1), slot)
+        for slot in (0, 1):
+            add_up(jnp.minimum(low + 2 * i + slot, high - 1), slot)
         return carry
 
     def apply(j, carry):
@@ -251,9 +252,7 @@
         u_ref[3, py, px, pz, at(j)] += delta_ref[6, at(j)]
         return carry
 
-    add_up(low)
-    lax.fori_loop(low + 1, high, work, 0)
-    change_row(high - 1)
+    lax.fori_loop(0, (high - low + 1) // 2 + 1, work, 0)
     lax.fori_loop(low, high, apply, 0)
 
 
@@ -331,7 +330,7 @@
 
 
 def coarse_sum(value):
-    return pair_sum(pair_sum(pair_sum(value, 1, 1), 0, 1), 0, 2)
+    return pair_sum(pair_sum(pair_sum(value, 1, 2), 0, 1), 0, 2)
 
 
 def cycle_weights(cells):
@@ -367,16 +366,24 @@
         viscous = jnp.where(viscous > 0, viscous, 1.0)
         for d in range(3):
             coarse = coarse_sum(sum_ref[d, y]) / viscous
-            smooth = weights[0] * coarse
-            for k in range(1, cells):
-                turned = pltpu.roll(coarse, sublanes - 4, 0)
-                coarse = jnp.where(number >= sublanes - 4, pltpu.roll(turned, HALF, 1), turned)
-                smooth = smooth + weights[k] * coarse
+            other = swapped(coarse)
+            smooth = weights[0] * coarse + weights[cells // 2] * other
+            for k in range(1, cells // 2):
+                near = pltpu.roll(coarse, sublanes - 4 * k, 0)
+                far = pltpu.roll(other, sublanes - 4 * k, 0)
+                inside = number < sublanes - 4 * k
+                smooth = smooth + weights[k] * jnp.where(inside, near, far)
+                smooth = smooth + weights[k + cells // 2] * jnp.where(inside, far, near)
             sum_ref[d, y] = coarse_gain * smooth
+
+    lane = lax.broadcasted_iota(jnp.int32, (SUBLANES, LANES), 1)
+    width = LANES - 2 * Z_MARGIN
+    spare = LANES - width
 
     def pack(j, carry):
         for py in (0, 1):
             for px in (0, 1):
+                first, second = [], []
                 for f in range(4):
                     even = u_ref[f, py, px, 0, at(Y_ROWS + j)]
                     odd = u_ref[f, py, px, 1, at(Y_ROWS + j)]
@@ -384,12 +391,16 @@
                         added = sum_ref[f, j // 2]
                         even = even + added
                         odd = odd + added
-                    low = lower_lanes(even.shape)
-                    first = jnp.where(low, even, pltpu.roll(odd, HALF, 1))
-                    second = jnp.where(low, pltpu.roll(even, HALF, 1), odd)
-                    for t in (0, 1):
-                        out_ref[t, f, py, j, px] = first[8 * t : 8 * t + 8]
-                        out_ref[t + 2, f, py, j, px] = second[8 * t : 8 * t + 8]
+                    low = even_lanes(even.shape)
+                    first.append(jnp.where(low, even, pltpu.roll(odd, 1, 1)))
+                    second.append(jnp.where(low, pltpu.roll(even, LANES - 1, 1), odd))
+                for f in range(3):
+                    for half, pieces in ((0, first), (2, second)):
+                        own = pltpu.roll(pieces[f], LANES - Z_MARGIN, 1)
+                        third = pltpu.roll(pieces[3], (width - Z_MARGIN - spare * f) % LANES, 1)
+                        tile = jnp.where(lane < width, own, third)
+                        for t in (0, 1):
+                            out_ref[t + half, f, py, j, px] = tile[8 * t : 8 * t + 8]
         return carry
 
     lax.fori_loop(0, rows, pack, 0)
@@ -397,8 +408,7 @@
 
 def refresh_pack_kernel(u_ref, left_ref, right_ref):
     rows = u_ref.shape[-2] // SUBLANES - 2 * Y_ROWS
-    pairs = Z_MARGIN // 2
-    lane = lax.broadcasted_iota(jnp.int32, (SUBLANES, LANES), 1) % HALF
+    place = lax.broadcasted_iota(jnp.int32, (SUBLANES, LANES), 1) // Z_MARGIN
 
     def one(j, carry):
         for py in (0, 1):
@@ -409,10 +419,10 @@
                     for pz in (0, 1):
                         slot = 2 * f + pz
                         value = u_ref[f, py, px, pz, at(Y_ROWS + j)]
-                        mine = (lane >= slot * pairs) & (lane < (slot + 1) * pairs)
-                        to_left = jnp.where(mine, pltpu.roll(value, (slot * pairs - pairs) % LANES, 1), to_left)
+                        shift = Z_MARGIN * slot
+                        to_left = jnp.where(place == slot, pltpu.roll(value, (shift - Z_MARGIN) % LANES, 1), to_left)
                         to_right = jnp.where(
-                            mine, pltpu.roll(value, (slot * pairs - (HALF - 2 * pairs)) % LANES, 1), to_right
+                            place == slot, pltpu.roll(value, (shift - LANES + 2 * Z_MARGIN) % LANES, 1), to_right
                         )
                 left_ref[py, j, px] = to_left
                 right_ref[py, j, px] = to_right
@@ -423,8 +433,7 @@
 
 def refresh_kernel(old_ref, from_left_ref, from_right_ref, u_ref, up_ref, down_ref):
     rows = u_ref.shape[-2] // SUBLANES - 2 * Y_ROWS
-    pairs = Z_MARGIN // 2
-    lane = lax.broadcasted_iota(jnp.int32, (SUBLANES, LANES), 1) % HALF
+    lane = lax.broadcasted_iota(jnp.int32, (SUBLANES, LANES), 1)
 
     def one(j, carry):
         for py in (0, 1):
@@ -433,13 +442,11 @@
                 high = from_right_ref[py, j, px]
                 for f in range(4):
                     for pz in (0, 1):
-                        slot = 2 * f + pz
+                        shift = Z_MARGIN * (2 * f + pz)
                         value = u_ref[f, py, px, pz, at(Y_ROWS + j)]
-                        value = jnp.where(lane < pairs, pltpu.roll(low, (-slot * pairs) % LANES, 1), value)
+                        value = jnp.where(lane < Z_MARGIN, pltpu.roll(low, (-shift) % LANES, 1), value)
                         value = jnp.where(
-                            lane >= HALF - pairs,
-                            pltpu.roll(high, (HALF - pairs - slot * pairs) % LANES, 1),
-                            value,
+                            lane >= LANES - Z_MARGIN, pltpu.roll(high, (-Z_MARGIN - shift) % LANES, 1), value
                         )
                         u_ref[f, py, px, pz, at(Y_ROWS + j)] = value
         return carry
@@ -453,82 +460,69 @@
     tiles = len(pieces)
     width = tiles * LANES // parts
     lane = lax.broadcasted_iota(jnp.int32, shape, 1)
-    order = 2 * (lane % HALF) + lane // HALF
-    pieces = [jnp.take_along_axis(piece, order, axis=1) for piece in pieces]
-    pair = lane % HALF
     for s in range(parts):
-        start = (width * s - Z_MARGIN) // 2
-        first, offset = start // HALF, start % HALF
+        start = width * s - Z_MARGIN
+        first, offset = start // LANES, start % LANES
         found = jnp.zeros(shape, jnp.float32)
         if 0 <= first < tiles:
-            found = jnp.where(pair < HALF - offset, pltpu.roll(pieces[first], (-offset) % LANES, 1), found)
+            found = jnp.where(lane < LANES - offset, pltpu.roll(pieces[first], (-offset) % LANES, 1), found)
         if 0 <= first + 1 < tiles:
-            found = jnp.where(pair >= HALF - offset, pltpu.roll(pieces[first + 1], (HALF - offset) % LANES, 1), found)
-        if width + 2 * Z_MARGIN < LANES:
-            found = jnp.where(pair < width // 2 + Z_MARGIN, found, 0.0)
+            found = jnp.where(lane >= LANES - offset, pltpu.roll(pieces[first + 1], (-offset) % LANES, 1), found)
         out_ref[(s,) + place] = found
 
 
-def pack_kernel(velocity_ref, pressure_ref, viscosity_ref, force_ref, out_ref, row_ref):
-    parts, _, _, rows = out_ref.shape[:4]
-    half = out_ref.shape[5]
+def pack_kernel(velocity_ref, pressure_ref, viscosity_ref, force_ref, state_ref, fixed_ref, row_ref):
+    parts = state_ref.shape[0]
+    half = state_ref.shape[5]
     tiles = row_ref.shape[2]
-
-    def one(j, carry):
-        for py in (0, 1):
-            y = 2 * j + py
-            for t in range(tiles):
-                columns = slice(LANES * t, LANES * (t + 1))
-                viscous = viscosity_ref[y, :, columns]
-                row_ref[py, 7, t] = viscous
-                row_ref[py, 3, t] = viscous * pressure_ref[y, :, columns]
-                for d in range(3):
-                    row_ref[py, d, t] = velocity_ref[d, y, :, columns]
-                    row_ref[py, 4 + d, t] = force_ref[d, y, :, columns]
-        for py in (0, 1):
-            for px in (0, 1):
-                for f in range(8):
-                    pieces = [row_ref[py, f, t, pl.ds(px, half, stride=2), :] for t in range(tiles)]
-                    cut_windows(pieces, out_ref, (f, py, j, px), parts)
-        return carry
-
-    lax.fori_loop(0, rows, one, 0)
+    for py in (0, 1):
+        for t in range(tiles):
+            columns = slice(LANES * t, LANES * (t + 1))
+            viscous = viscosity_ref[py, :, columns]
+            row_ref[py, 7, t] = viscous
+            row_ref[py, 3, t] = viscous * pressure_ref[py, :, columns]
+            for d in range(3):
+                row_ref[py, d, t] = velocity_ref[d, py, :, columns]
+                row_ref[py, 4 + d, t] = force_ref[d, py, :, columns]
+    for py in (0, 1):
+        for px in (0, 1):
+            for f in range(8):
+                pieces = [row_ref[py, f, t, pl.ds(px, half, stride=2), :] for t in range(tiles)]
+                cut_windows(pieces, state_ref if f < 4 else fixed_ref, (f % 4, py, 0, px), parts)
 
 
 def unpack_kernel(back_ref, viscosity_ref, velocity_ref, pressure_ref, row_ref):
-    parts, fields, _, rows = back_ref.shape[:4]
+    parts = back_ref.shape[0]
     tiles = row_ref.shape[2]
     width = tiles * LANES // parts
+    spare = LANES - width
     shape = back_ref.shape[-2:]
     lane = lax.broadcasted_iota(jnp.int32, shape, 1)
-    order = HALF * (lane % 2) + lane // 2
-
-    def one(j, carry):
-        for py in (0, 1):
-            for px in (0, 1):
-                for f in range(fields):
-                    pieces = [jnp.zeros(shape, jnp.float32)] * tiles
-                    for s in range(parts):
-                        start = width * s - Z_MARGIN
-                        found = jnp.take_along_axis(back_ref[s, f, py, j, px], order, axis=1)
-                        found = pltpu.roll(found, start % LANES, 1)
-                        for t in range(tiles):
-                            low = max(width * s - LANES * t, 0)
-                            high = min(width * (s + 1) - LANES * t, LANES)
-                            if low < high:
-                                pieces[t] = jnp.where((lane >= low) & (lane < high), found, pieces[t])
-                    for t, piece in enumerate(pieces):
-                        row_ref[py, f, t, pl.ds(px, shape[0], stride=2), :] = piece
-        for py in (0, 1):
-            y = 2 * j + py
-            for t in range(tiles):
-                columns = slice(LANES * t, LANES * (t + 1))
-                for d in range(3):
-                    velocity_ref[d, y, :, columns] = row_ref[py, d, t]
-                pressure_ref[y, :, columns] = row_ref[py, 3, t] / viscosity_ref[y, :, columns]
-        return carry
-
-    lax.fori_loop(0, rows, one, 0)
+    for py in (0, 1):
+        for px in (0, 1):
+            pieces = [[jnp.zeros(shape, jnp.float32)] * tiles for f in range(4)]
+            for s in range(parts):
+                got = [back_ref[s, f, py, 0, px] for f in range(3)]
+                pressure = jnp.zeros(shape, jnp.float32)
+                for f in range(3):
+                    third = pltpu.roll(got[f], (spare * f - width) % LANES, 1)
+                    pressure = jnp.where(lane // spare == f, third, pressure)
+                for f, found in enumerate(got + [pressure]):
+                    found = pltpu.roll(found, width * s % LANES, 1)
+                    for t in range(tiles):
+                        low = max(width * s - LANES * t, 0)
+                        high = min(width * (s + 1) - LANES * t, LANES)
+                        if low < high:
+                            pieces[f][t] = jnp.where((lane >= low) & (lane < high), found, pieces[f][t])
+            for f in range(4):
+                for t in range(tiles):
+                    row_ref[py, f, t, pl.ds(px, shape[0], stride=2), :] = pieces[f][t]
+    for py in (0, 1):
+        for t in range(tiles):
+            columns = slice(LANES * t, LANES * (t + 1))
+            for d in range(3):
+                velocity_ref[d, py, :, columns] = row_ref[py, d, t]
+            pressure_ref[py, :, columns] = row_ref[py, 3, t] / viscosity_ref[py, :, columns]
 
 
 def shaped(*shape):
@@ -562,26 +556,42 @@
     tile = (SUBLANES, LANES)
     own = shaped(4, 2, rows, 2, 2, *tile)
     strip = shaped(4, 2, Y_ROWS, 2, 2, *tile)
-    sent = pl.pallas_call(
+    sent = shaped(parts, 4, 2, rows, 2, lon_cells // 2, LANES)
+    sent_block = pl.BlockSpec((parts, 4, 2, 1, 2, lon_cells // 2, LANES), lambda j: (0, 0, 0, j, 0, 0, 0))
+    state_sent, fixed_sent = pl.pallas_call(
         pack_kernel,
-        out_shape=shaped(parts, 8, 2, rows, 2, lon_cells // 2, LANES),
-        in_specs=[VMEM] * 4,
-        out_specs=VMEM,
+        out_shape=(sent, sent),
+        grid=(rows,),
+        in_specs=[
+            pl.BlockSpec((3, 2, lon_cells, rad_cells), lambda j: (0, j, 0, 0)),
+            pl.BlockSpec((2, lon_cells, rad_cells), lambda j: (j, 0, 0)),
+            pl.BlockSpec((2, lon_cells, rad_cells), lambda j: (j, 0, 0)),
+            pl.BlockSpec((3, 2, lon_cells, rad_cells), lambda j: (0, j, 0, 0)),
+        ],
+        out_specs=(sent_block, sent_block),
         scratch_shapes=[pltpu.VMEM((2, 8, rad_cells // LANES, lon_cells, LANES), jnp.float32)],
         compiler_params=params(16),
-    )(
-        velocity.transpose(0, 2, 1, 3), pressure_in.transpose(1, 0, 2),
-        viscosity.transpose(1, 0, 2), body_force.transpose(0, 2, 1, 3),
-    )
-    got = lax.all_to_all(sent, "lon", 0, 0, tiled=True)
-    own_state, state_up, state_down, own_fixed, fixed_up, fixed_down = pl.pallas_call(
-        assemble_kernel,
-        out_shape=(own, strip, strip) * 2,
-        in_specs=[VMEM],
-        out_specs=(VMEM,) * 6,
-        compiler_params=params(16),
-    )(got)
+    )(*[
+        pltpu.with_memory_space_constraint(array, pltpu.HBM)
+        for array in (
+            velocity.transpose(0, 2, 1, 3), pressure_in.transpose(1, 0, 2),
+            viscosity.transpose(1, 0, 2), body_force.transpose(0, 2, 1, 3),
+        )
+    ])
+
+    def assembled(pieces):
+        return pl.pallas_call(
+            assemble_kernel,
+            out_shape=(own, strip, strip),
+            in_specs=[VMEM],
+            out_specs=(VMEM, VMEM, VMEM),
+            compiler_params=params(12),
+        )(lax.all_to_all(pieces, "lon", 0, 0, tiled=True))
+
+    own_fixed, fixed_up, fixed_down = assembled(fixed_sent)
+    fixed_up, fixed_down, state_sent = lax.optimization_barrier((fixed_up, fixed_down, state_sent))
     fixed_below, fixed_above = exchange(fixed_up, fixed_down, "lat", lats)
+    own_state, state_up, state_down = assembled(state_sent)
     below, above = exchange(state_up, state_down, "lat", lats)
     stacked = (2, 2, 2)
     *couplings, diagonals, force, viscous_sum = pl.pallas_call(
@@ -601,7 +611,7 @@
     state_type = kept(4, *stacked, pitch(total), LANES)
     scratch = [
         pltpu.VMEM((7, pitch(total), LANES), jnp.float32),
-        pltpu.VMEM((6, 4) + tile, jnp.float32),
+        pltpu.VMEM((2, 6, 4) + tile, jnp.float32),
     ]
     state, up, down = pl.pallas_call(
         first_kernel,
@@ -643,7 +653,7 @@
     below, above = exchange(up, down, "lat", lats)
     state, packed = pl.pallas_call(
         final_kernel,
-        out_shape=(state_type, shaped(parts, 4, 2, rows, 2, lon_cells // 2, LANES)),
+        out_shape=(state_type, shaped(parts, 3, 2, rows, 2, lon_cells // 2, LANES)),
         in_specs=[SMEM] + [VMEM] * 14,
         out_specs=(VMEM, VMEM),
         scratch_shapes=scratch + [pltpu.VMEM((3, rows // 2) + tile, jnp.float32)],
@@ -654,8 +664,15 @@
     velocity_out, pressure_out = pl.pallas_call(
         unpack_kernel,
         out_shape=(shaped(3, lat_cells, lon_cells, rad_cells), shaped(lat_cells, lon_cells, rad_cells)),
-        in_specs=[VMEM, VMEM],
-        out_specs=(VMEM, VMEM),
+        grid=(rows,),
+        in_specs=[
+            pl.BlockSpec((parts, 3, 2, 1, 2, lon_cells // 2, LANES), lambda j: (0, 0, 0, j, 0, 0, 0)),
+            pl.BlockSpec((2, lon_cells, rad_cells), lambda j: (j, 0, 0)),
+        ],
+        out_specs=(
+            pl.BlockSpec((3, 2, lon_cells, rad_cells), lambda j: (0, j, 0, 0)),
+            pl.BlockSpec((2, lon_cells, rad_cells), lambda j: (j, 0, 0)),
+        ),
         scratch_shapes=[pltpu.VMEM((2, 4, rad_cells // LANES, lon_cells, LANES), jnp.float32)],
         compiler_params=params(16),
     )(back, viscosity.transpose(1, 0, 2))
@@ -853,9 +870,7 @@
         and lat_cells % 4 == 0
         and lat_cells >= 2 * Y_ROWS
         and rad_cells % LANES == 0
-        and rad_cells % (4 * parts) == 0
-        and rad_cells // parts + 2 * Z_MARGIN <= LANES
-        and Z_MARGIN <= rad_cells // parts
+        and rad_cells // parts + 2 * Z_MARGIN == LANES
     )
     chosen = body_windows if fits else body_general
     return chosen(velocity, pressure_in, viscosity, body_force, colour_order)

time: 242 us -> 217 us (0.90)
  blocking collectives: 60.3 us -> 39.1 us
  Pallas kernels: 83.1 us -> 73.4 us
  starting transfers between devices: 30.3 us -> 35.3 us
  waiting for transfers between devices: 61.7 us -> 66 us
    all_to_all x1, blocking collectives: 38.6 us -> 21.7 us  [assembled(): lax.all_to_all(pieces, 'lon', 0, 0, tiled=True)]
    all_to_all x0 -> x1, waiting for transfers between devices: none -> 11.4 us  [assembled(): lax.all_to_all(pieces, 'lon', 0, 0, tiled=True)]
    pallas_call x3 -> x4, Pallas kernels: 29.9 us -> 23.8 us  [the longest x1 17.5 us: body_windows(): pl.pallas_call(final_kernel, out_shape=(state_type, shaped(parts, 3, 2, r...]
    all_to_all x1, blocking collectives: 21.7 us -> 17.4 us  [body_windows(): back = lax.all_to_all(packed, 'lon', 0, 0, tiled=True)]
    ppermute x6, waiting for transfers between devices: 35 us -> 31 us  [exchange(): below = lax.ppermute(value_up, axis, [(i, i + 1) for i in range(count - 1)])]
    all_to_all x0 -> x1, starting transfers between devices: none -> 3.56 us  [assembled(): lax.all_to_all(pieces, 'lon', 0, 0, tiled=True)]
    pallas_call x2, Pallas kernels: 27 us -> 23.7 us  [body_windows(): pl.pallas_call(functools.partial(sweep_kernel, g), out_shape=(state_type,...]
    ppermute x6, waiting for transfers between devices: 26.7 us -> 23.6 us  [exchange(): lax.ppermute(value_down, axis, [(i + 1, i) for i in range(count - 1)])]
  transfers between devices with their start and end apart: 12 -> 13, of which waited for: 11 -> 11; matrix products, arithmetic and copies ran while one was open for 0% -> 0% of each run, Pallas kernels for 3% -> 5%
where the time goes in v2:
time: 217 us
  Pallas kernels  73.4 us (34%)
  waiting for transfers between devices  66 us (30%)
  blocking collectives  39.1 us (18%)
  starting transfers between devices  35.3 us (16%)
    ppermute x6, waiting for transfers between devices, exchange(): below = lax.ppermute(value_up, axis, [(i, i + 1) for i in range(count - 1)])  31 us
    pallas_call x2, Pallas kernels, body_windows(): pl.pallas_call(functools.partial(sweep_kernel, g), out_shape=(state_type,...  23.7 us
    ppermute x6, waiting for transfers between devices, exchange(): lax.ppermute(value_down, axis, [(i + 1, i) for i in range(count - 1)])  23.6 us
    all_to_all x1, blocking collectives, assembled(): lax.all_to_all(pieces, 'lon', 0, 0, tiled=True)  21.7 us
    ppermute x6, starting transfers between devices, exchange(): below = lax.ppermute(value_up, axis, [(i, i + 1) for i in range(count - 1)])  19.9 us
    pallas_call x1, Pallas kernels, body_windows(): pl.pallas_call(final_kernel, out_shape=(state_type, shaped(parts, 3, 2, r...  17.5 us
    all_to_all x1, blocking collectives, body_windows(): back = lax.all_to_all(packed, 'lon', 0, 0, tiled=True)  17.4 us
    ppermute x6, starting transfers between devices, exchange(): lax.ppermute(value_down, axis, [(i + 1, i) for i in range(count - 1)])  11.9 us
  transfers between devices with their start and end apart: 13, of which 11 were waited for; matrix products, arithmetic and copies ran while one was open for 0% of the time, Pallas kernels for 5%

profile of v2, /device:TPU:9, one launch (start us, length us, event | category | flops | bytes accessed | tf_op | source)
XLA Modules:
  0.0 216.7 jit_solution(11164042365968339572)
XLA Ops:
  0.6 4.4 %shard_map.68 = (f32[4,4,2,6,2,8,128]{6,5,4,3,2,1,0:T(8,128)S(1)}, f32[4,4,2,6,2,8,128]{6,5,4,3,2,1,0:T(8,128)S(1)}) custom-call(f32[3,12,16,384]{3,2,1,0:T(8,128)} %bitcast.8, f32[12,16,384]{2,1,0:T(8,128)} %bitcast.10, f32[12,16,384]{2,1,0:T(8,128)} %bitcast.6, f32[3,12,16,384]{3,2,1,0:T(8,128)} %bitcast.9), custom_call_target="tpu_custom_call" | custom-call | tf_op jit(solution)/shard_map/pallas_call | solution.py:561
  5.1 21.7 %all_to_all.15.in_ref = f32[4,4,2,6,2,8,128]{6,5,4,3,2,1,0:T(8,128)S(1)} all-to-all(f32[4,4,2,6,2,8,128]{6,5,4,3,2,1,0:T(8,128)S(1)} %get-tuple-element.39), channel_id=1, replica_groups=mesh['lon'=4,'lat'=8] {'lon'}, dimensions={0} | all-to-all | bytes 3145728 | tf_op jit(solution)/shard_map/all_to_all | solution.py:589
  29.8 3.6 %all-to-all-start.1 = ((f32[4,4,2,6,2,8,128]{6,5,4,3,2,1,0:T(8,128)}), f32[4,4,2,6,2,8,128]{6,5,4,3,2,1,0:T(8,128)S(1)}, u32[]{:S(2)}, u32[]{:S(2)}) async-start(f32[4,4,2,6,2,8,128]{6,5,4,3,2,1,0:T(8,128)} %copy-done), calls=%async_computation.1 | async-start | bytes 3145728 | tf_op jit(solution)/shard_map/all_to_all | solution.py:589
  33.4 5.3 %collective-permute-start.2 = (f32[4,2,4,2,2,16,128]{6,5,4,3,2,1,0:T(8,128)}, f32[4,2,4,2,2,16,128]{6,5,4,3,2,1,0:T(8,128)}, u32[]{:S(2)}, u32[]{:S(2)}) collective-permute-start(f32[4,2,4,2,2,16,128]{6,5,4,3,2,1,0:T(8,128)} %copy-done.4), channel_id=1, source_target_pairs={{0,1},{1,2},{2,3},{3,4},{4,5},{5,6},{6,7},{8,9},{9,10},{10,11},{11... | collective-permute-start | bytes 3145736 | tf_op jit(solution)/shard_map/ppermute | solution.py:545
  40.6 11.4 %all-to-all-done.1.in_ref = f32[4,4,2,6,2,8,128]{6,5,4,3,2,1,0:T(8,128)S(1)} async-done(((f32[4,4,2,6,2,8,128]{6,5,4,3,2,1,0:T(8,128)}), f32[4,4,2,6,2,8,128]{6,5,4,3,2,1,0:T(8,128)S(1)}, u32[]{:S(2)}, u32[]{:S(2)}) %all-to-all-start.1) | async-done | bytes 1572896 | tf_op jit(solution)/shard_map/all_to_all | solution.py:589
  53.0 4.6 %collective-permute-start = (f32[4,2,4,2,2,16,128]{6,5,4,3,2,1,0:T(8,128)S(1)}, f32[4,2,4,2,2,16,128]{6,5,4,3,2,1,0:T(8,128)S(1)}, u32[]{:S(2)}, u32[]{:S(2)}) collective-permute-start(f32[4,2,4,2,2,16,128]{6,5,4,3,2,1,0:T(8,128)S(1)} %get-tuple-element.45), channel_id=1, source_target_pairs={{0,1},{1,2},{2,3},{3,4},{4,5},{5,6},{6,7},{8,9},{9,10},{10,11},{11... | collective-permute-start | bytes 3145736 | tf_op jit(solution)/shard_map/ppermute | solution.py:545
  59.5 9.5 %shard_map.71 = (f32[26,232,128]{2,1,0:T(8,128)S(1)}, f32[26,232,128]{2,1,0:T(8,128)S(1)}, f32[26,232,128]{2,1,0:T(8,128)S(1)}, f32[26,232,128]{2,1,0:T(8,128)S(...) custom-call(f32[4,2,6,2,2,16,128]{6,5,4,3,2,1,0:T(8,128)S(1)} %get-t, ...), custom_call_target="tpu_custom_call" | custom-call | tf_op jit(solution)/shard_map/pallas_call | solution.py:597
  69.3 4.4 %collective-permute-done.1.above_ref = f32[4,2,4,2,2,16,128]{6,5,4,3,2,1,0:T(8,128)S(1)} collective-permute-done((f32[4,2,4,2,2,16,128]{6,5,4,3,2,1,0:T(8,128)S(1)}, f32[4,2,4,2,2,16,128]{6,5,4,3,2,1,0:T(8,128)S(1)}, u32[]{:S(2)}, u32[]{:S(2)}) %collective-permute-start.1) | collective-permute-done | bytes 1048608 | tf_op jit(solution)/shard_map/ppermute | solution.py:546
  73.7 11.1 %shard_map.72 = (f32[4,2,2,2,232,128]{5,4,3,2,1,0:T(8,128)S(1)}, f32[4,2,4,2,2,16,128]{6,5,4,3,2,1,0:T(8,128)S(1)}, f32[4,2,4,2,2,16,128]{6,5,4,3,2,1,0:T(8,128)S(1)}) custom-call(s32[8]{0:T(128)S(1)} %copy-done.2, f32[4,2,6,2,2,16,128]{6,5,4,3,2,1,0:T(8,128)S(1)} %get-tuple-element.44.own_ref, ...), custom_call_target="tpu_custom_call" | custom-call | tf_op jit(solution)/shard_map/pallas_call | solution.py:616
  89.2 9.3 %collective-permute-done.4.below_ref = f32[4,2,4,2,2,16,128]{6,5,4,3,2,1,0:T(8,128)S(1)} collective-permute-done((f32[4,2,4,2,2,16,128]{6,5,4,3,2,1,0:T(8,128)S(1)}, f32[4,2,4,2,2,16,128]{6,5,4,3,2,1,0:T(8,128)S(1)}, u32[]{:S(2)}, u32[]{:S(2)}) %collective-permute-start.4) | collective-permute-done | bytes 1048608 | tf_op jit(solution)/shard_map/ppermute | solution.py:545
  98.5 4.4 %collective-permute-done.5.above_ref = f32[4,2,4,2,2,16,128]{6,5,4,3,2,1,0:T(8,128)S(1)} collective-permute-done((f32[4,2,4,2,2,16,128]{6,5,4,3,2,1,0:T(8,128)S(1)}, f32[4,2,4,2,2,16,128]{6,5,4,3,2,1,0:T(8,128)S(1)}, u32[]{:S(2)}, u32[]{:S(2)}) %collective-permute-start.5) | collective-permute-done | bytes 1048608 | tf_op jit(solution)/shard_map/ppermute | solution.py:546
  102.9 12.6 %shard_map.73 = (f32[4,2,2,2,232,128]{5,4,3,2,1,0:T(8,128)S(1)}, f32[4,2,4,2,2,16,128]{6,5,4,3,2,1,0:T(8,128)}, f32[4,2,4,2,2,16,128]{6,5,4,3,2,1,0:T(8,128)}) custom-call(s32[8]{0:T(128)S(1)} %copy-done.2, f32[4,2,2,2,232,128]{5,4,3,2,1,0:T(8,128)S(1)} %get-tuple-element.60.old_ref, ...), custom_call_target="tpu_custom_call", output_to_operand_aliasing={{0}: (1, {})} | custom-call | tf_op jit(solution)/shard_map/pallas_call | solution.py:626
  116.6 3.1 %collective-permute-start.6 = (f32[2,6,2,16,128]{4,3,2,1,0:T(8,128)S(1)}, f32[2,6,2,16,128]{4,3,2,1,0:T(8,128)S(1)}, u32[]{:S(2)}, u32[]{:S(2)}) collective-permute-start(f32[2,6,2,16,128]{4,3,2,1,0:T(8,128)S(1)} %get-tuple-element.64), channel_id=1, source_target_pairs={{0,8},{8,16},{16,24},{1,9},{9,17},{17,25},{2,10},{10,18},{18,26},{... | collective-permute-start | bytes 589832 | tf_op jit(solution)/shard_map/ppermute | solution.py:545
  121.0 2.5 %collective-permute-done.6.from_left_ref = f32[2,6,2,16,128]{4,3,2,1,0:T(8,128)S(1)} collective-permute-done((f32[2,6,2,16,128]{4,3,2,1,0:T(8,128)S(1)}, f32[2,6,2,16,128]{4,3,2,1,0:T(8,128)S(1)}, u32[]{:S(2)}, u32[]{:S(2)}) %collective-permute-start.6) | collective-permute-done | bytes 196640 | tf_op jit(solution)/shard_map/ppermute | solution.py:545
  123.5 5.9 %collective-permute-done.7.from_right_ref = f32[2,6,2,16,128]{4,3,2,1,0:T(8,128)S(1)} collective-permute-done((f32[2,6,2,16,128]{4,3,2,1,0:T(8,128)S(1)}, f32[2,6,2,16,128]{4,3,2,1,0:T(8,128)S(1)}, u32[]{:S(2)}, u32[]{:S(2)}) %collective-permute-start.7) | collective-permute-done | bytes 196640 | tf_op jit(solution)/shard_map/ppermute | solution.py:546
  130.7 2.9 %collective-permute-start.8 = (f32[4,2,4,2,2,16,128]{6,5,4,3,2,1,0:T(8,128)S(1)}, f32[4,2,4,2,2,16,128]{6,5,4,3,2,1,0:T(8,128)S(1)}, u32[]{:S(2)}, u32[]{:S(2)}) collective-permute-start(f32[4,2,4,2,2,16,128]{6,5,4,3,2,1,0:T(8,128)S(1)} %get-tuple-element.67), channel_id=1, source_target_pairs={{0,1},{1,2},{2,3},{3,4},{4,5},{5,6},{6,7},{8,9},{9,10},{10,11},{11... | collective-permute-start | bytes 3145736 | tf_op jit(solution)/shard_map/ppermute | solution.py:545
  135.5 9.8 %collective-permute-done.8.below_ref = f32[4,2,4,2,2,16,128]{6,5,4,3,2,1,0:T(8,128)S(1)} collective-permute-done((f32[4,2,4,2,2,16,128]{6,5,4,3,2,1,0:T(8,128)S(1)}, f32[4,2,4,2,2,16,128]{6,5,4,3,2,1,0:T(8,128)S(1)}, u32[]{:S(2)}, u32[]{:S(2)}) %collective-permute-start.8) | collective-permute-done | bytes 1048608 | tf_op jit(solution)/shard_map/ppermute | solution.py:545
  145.3 4.4 %collective-permute-done.9.above_ref = f32[4,2,4,2,2,16,128]{6,5,4,3,2,1,0:T(8,128)S(1)} collective-permute-done((f32[4,2,4,2,2,16,128]{6,5,4,3,2,1,0:T(8,128)S(1)}, f32[4,2,4,2,2,16,128]{6,5,4,3,2,1,0:T(8,128)S(1)}, u32[]{:S(2)}, u32[]{:S(2)}) %collective-permute-start.9) | collective-permute-done | bytes 1048608 | tf_op jit(solution)/shard_map/ppermute | solution.py:546
  149.7 11.0 %shard_map.76 = (f32[4,2,2,2,232,128]{5,4,3,2,1,0:T(8,128)S(1)}, f32[4,2,4,2,2,16,128]{6,5,4,3,2,1,0:T(8,128)S(1)}, f32[4,2,4,2,2,16,128]{6,5,4,3,2,1,0:T(8,128)S(1)}) custom-call(s32[8]{0:T(128)S(1)} %copy-done.2, f32[4,2,2,2,232,128]{5,4,3,2,1,0:T(8,128)S(1)} %get-tuple-element.66.old_ref, ...), custom_call_target="tpu_custom_call", output_to_operand_aliasing={{0}: (1, {})} | custom-call | tf_op jit(solution)/shard_map/pallas_call | solution.py:626
  165.2 9.1 %collective-permute-done.10.below_ref = f32[4,2,4,2,2,16,128]{6,5,4,3,2,1,0:T(8,128)S(1)} collective-permute-done((f32[4,2,4,2,2,16,128]{6,5,4,3,2,1,0:T(8,128)S(1)}, f32[4,2,4,2,2,16,128]{6,5,4,3,2,1,0:T(8,128)S(1)}, u32[]{:S(2)}, u32[]{:S(2)}) %collective-permute-start.10) | collective-permute-done | bytes 1048608 | tf_op jit(solution)/shard_map/ppermute | solution.py:545
  174.4 4.6 %collective-permute-done.11.above_ref = f32[4,2,4,2,2,16,128]{6,5,4,3,2,1,0:T(8,128)S(1)} collective-permute-done((f32[4,2,4,2,2,16,128]{6,5,4,3,2,1,0:T(8,128)S(1)}, f32[4,2,4,2,2,16,128]{6,5,4,3,2,1,0:T(8,128)S(1)}, u32[]{:S(2)}, u32[]{:S(2)}) %collective-permute-start.11) | collective-permute-done | bytes 1048608 | tf_op jit(solution)/shard_map/ppermute | solution.py:546
  178.9 17.5 %shard_map.77 = (f32[4,2,2,2,232,128]{5,4,3,2,1,0:T(8,128)S(1)}, f32[4,3,2,6,2,8,128]{6,5,4,3,2,1,0:T(8,128)S(1)}) custom-call(s32[8]{0:T(128)S(1)} %copy-done.2, f32[4,2,2,2,232,128]{5,4,3,2,1,0:T(8,128)S(1)} %get-tuple-element.69.old_ref, f32[4,2,4,2,2,16,128]{6,5,4,3,2,1,0:T(8,128)S(1)} %collective-permute-done.10.below_ref, ...), custom_call_target="tpu_custom_call", output_to_operand_aliasing={{0}: (1, {})} | custom-call | tf_op jit(solution)/shard_map/pallas_call | solution.py:654
  196.4 17.4 %all_to_all.16.back_ref = f32[4,3,2,6,2,8,128]{6,5,4,3,2,1,0:T(8,128)S(1)} all-to-all(f32[4,3,2,6,2,8,128]{6,5,4,3,2,1,0:T(8,128)S(1)} %get-tuple-element.73), channel_id=1, replica_groups=mesh['lon'=4,'lat'=8] {'lon'}, dimensions={0} | all-to-all | bytes 2359296 | tf_op jit(solution)/shard_map/all_to_all | solution.py:663
  213.8 2.9 %shard_map.78 = (f32[3,12,16,384]{3,2,1,0:T(8,128)}, f32[12,16,384]{2,1,0:T(8,128)}) custom-call(f32[4,3,2,6,2,8,128]{6,5,4,3,2,1,0:T(8,128)S(1)} %all_to_all.16.back_ref, f32[12,16,384]{2,1,0:T(8,128)S(1)} %bitcast.7), custom_call_target="tpu_custom_call" | custom-call | tf_op jit(solution)/shard_map/pallas_call | solution.py:664
  (25 shorter events, 22.4 us)
Async XLA Ops:
  5.1 24.7 %copy-start = (f32[4,4,2,6,2,8,128]{6,5,4,3,2,1,0:T(8,128)}, f32[4,4,2,6,2,8,128]{6,5,4,3,2,1,0:T(8,128)S(1)}, u32[]{:S(2)}) copy-start(f32[4,4,2,6,2,8,128]{6,5,4,3,2,1,0:T(8,128)S(1)} %get-tuple-element.43) | copy-start | bytes 4718596
  27.8 1.0 copy-start.3
  28.8 1.0 copy-start.4
  29.8 22.2 %all-to-all-start.1 = ((f32[4,4,2,6,2,8,128]{6,5,4,3,2,1,0:T(8,128)}), f32[4,4,2,6,2,8,128]{6,5,4,3,2,1,0:T(8,128)S(1)}, u32[]{:S(2)}, u32[]{:S(2)}) async-start(f32[4,4,2,6,2,8,128]{6,5,4,3,2,1,0:T(8,128)} %copy-done), calls=%async_computation.1 | async-start | bytes 3145728 | tf_op jit(solution)/shard_map/all_to_all | solution.py:589
  33.4 40.3 %copy-start.2 = (s32[8]{0:T(128)S(1)}, s32[8]{0:T(128)}, u32[]{:S(2)}) copy-start(s32[8]{0:T(128)} %order_ref.7) | copy-start | bytes 100
  33.4 26.1 %collective-permute-start.2 = (f32[4,2,4,2,2,16,128]{6,5,4,3,2,1,0:T(8,128)}, f32[4,2,4,2,2,16,128]{6,5,4,3,2,1,0:T(8,128)}, u32[]{:S(2)}, u32[]{:S(2)}) collective-permute-start(f32[4,2,4,2,2,16,128]{6,5,4,3,2,1,0:T(8,128)} %copy-done.4), channel_id=1, source_target_pairs={{0,1},{1,2},{2,3},{3,4},{4,5},{5,6},{6,7},{8,9},{9,10},{10,11},{11... | collective-permute-start | bytes 3145736 | tf_op jit(solution)/shard_map/ppermute | solution.py:545
  38.7 20.8 %collective-permute-start.3 = (f32[4,2,4,2,2,16,128]{6,5,4,3,2,1,0:T(8,128)}, f32[4,2,4,2,2,16,128]{6,5,4,3,2,1,0:T(8,128)}, u32[]{:S(2)}, u32[]{:S(2)}) collective-permute-start(f32[4,2,4,2,2,16,128]{6,5,4,3,2,1,0:T(8,128)} %copy-done.3), channel_id=1, source_target_pairs={{1,0},{2,1},{3,2},{4,3},{5,4},{6,5},{7,6},{9,8},{10,9},{11,10},{12... | collective-permute-start | bytes 3145736 | tf_op jit(solution)/shard_map/ppermute | solution.py:546
  53.0 16.3 %collective-permute-start = (f32[4,2,4,2,2,16,128]{6,5,4,3,2,1,0:T(8,128)S(1)}, f32[4,2,4,2,2,16,128]{6,5,4,3,2,1,0:T(8,128)S(1)}, u32[]{:S(2)}, u32[]{:S(2)}) collective-permute-start(f32[4,2,4,2,2,16,128]{6,5,4,3,2,1,0:T(8,128)S(1)} %get-tuple-element.45), channel_id=1, source_target_pairs={{0,1},{1,2},{2,3},{3,4},{4,5},{5,6},{6,7},{8,9},{9,10},{10,11},{11... | collective-permute-start | bytes 3145736 | tf_op jit(solution)/shard_map/ppermute | solution.py:545
  57.6 16.1 %collective-permute-start.1 = (f32[4,2,4,2,2,16,128]{6,5,4,3,2,1,0:T(8,128)S(1)}, f32[4,2,4,2,2,16,128]{6,5,4,3,2,1,0:T(8,128)S(1)}, u32[]{:S(2)}, u32[]{:S(2)}) collective-permute-start(f32[4,2,4,2,2,16,128]{6,5,4,3,2,1,0:T(8,128)S(1)} %get-tuple-element.46), channel_id=1, source_target_pairs={{1,0},{2,1},{3,2},{4,3},{5,4},{6,5},{7,6},{9,8},{10,9},{11,10},{12... | collective-permute-start | bytes 3145736 | tf_op jit(solution)/shard_map/ppermute | solution.py:546
  84.8 13.7 %collective-permute-start.4 = (f32[4,2,4,2,2,16,128]{6,5,4,3,2,1,0:T(8,128)S(1)}, f32[4,2,4,2,2,16,128]{6,5,4,3,2,1,0:T(8,128)S(1)}, u32[]{:S(2)}, u32[]{:S(2)}) collective-permute-start(f32[4,2,4,2,2,16,128]{6,5,4,3,2,1,0:T(8,128)S(1)} %get-tuple-element.61), channel_id=1, source_target_pairs={{0,1},{1,2},{2,3},{3,4},{4,5},{5,6},{6,7},{8,9},{9,10},{10,11},{11... | collective-permute-start | bytes 3145736 | tf_op jit(solution)/shard_map/ppermute | solution.py:545
  86.7 16.1 %collective-permute-start.5 = (f32[4,2,4,2,2,16,128]{6,5,4,3,2,1,0:T(8,128)S(1)}, f32[4,2,4,2,2,16,128]{6,5,4,3,2,1,0:T(8,128)S(1)}, u32[]{:S(2)}, u32[]{:S(2)}) collective-permute-start(f32[4,2,4,2,2,16,128]{6,5,4,3,2,1,0:T(8,128)S(1)} %get-tuple-element.62), channel_id=1, source_target_pairs={{1,0},{2,1},{3,2},{4,3},{5,4},{6,5},{7,6},{9,8},{10,9},{11,10},{12... | collective-permute-start | bytes 3145736 | tf_op jit(solution)/shard_map/ppermute | solution.py:546
  116.6 6.9 %collective-permute-start.6 = (f32[2,6,2,16,128]{4,3,2,1,0:T(8,128)S(1)}, f32[2,6,2,16,128]{4,3,2,1,0:T(8,128)S(1)}, u32[]{:S(2)}, u32[]{:S(2)}) collective-permute-start(f32[2,6,2,16,128]{4,3,2,1,0:T(8,128)S(1)} %get-tuple-element.64), channel_id=1, source_target_pairs={{0,8},{8,16},{16,24},{1,9},{9,17},{17,25},{2,10},{10,18},{18,26},{... | collective-permute-start | bytes 589832 | tf_op jit(solution)/shard_map/ppermute | solution.py:545
  119.7 9.7 %collective-permute-start.7 = (f32[2,6,2,16,128]{4,3,2,1,0:T(8,128)S(1)}, f32[2,6,2,16,128]{4,3,2,1,0:T(8,128)S(1)}, u32[]{:S(2)}, u32[]{:S(2)}) collective-permute-start(f32[2,6,2,16,128]{4,3,2,1,0:T(8,128)S(1)} %get-tuple-element.65), channel_id=1, source_target_pairs={{8,0},{16,8},{24,16},{9,1},{17,9},{25,17},{10,2},{18,10},{26,18},{... | collective-permute-start | bytes 589832 | tf_op jit(solution)/shard_map/ppermute | solution.py:546
  130.7 14.6 %collective-permute-start.8 = (f32[4,2,4,2,2,16,128]{6,5,4,3,2,1,0:T(8,128)S(1)}, f32[4,2,4,2,2,16,128]{6,5,4,3,2,1,0:T(8,128)S(1)}, u32[]{:S(2)}, u32[]{:S(2)}) collective-permute-start(f32[4,2,4,2,2,16,128]{6,5,4,3,2,1,0:T(8,128)S(1)} %get-tuple-element.67), channel_id=1, source_target_pairs={{0,1},{1,2},{2,3},{3,4},{4,5},{5,6},{6,7},{8,9},{9,10},{10,11},{11... | collective-permute-start | bytes 3145736 | tf_op jit(solution)/shard_map/ppermute | solution.py:545
  133.6 16.1 %collective-permute-start.9 = (f32[4,2,4,2,2,16,128]{6,5,4,3,2,1,0:T(8,128)S(1)}, f32[4,2,4,2,2,16,128]{6,5,4,3,2,1,0:T(8,128)S(1)}, u32[]{:S(2)}, u32[]{:S(2)}) collective-permute-start(f32[4,2,4,2,2,16,128]{6,5,4,3,2,1,0:T(8,128)S(1)} %get-tuple-element.68), channel_id=1, source_target_pairs={{1,0},{2,1},{3,2},{4,3},{5,4},{6,5},{7,6},{9,8},{10,9},{11,10},{12... | collective-permute-start | bytes 3145736 | tf_op jit(solution)/shard_map/ppermute | solution.py:546
  160.7 13.7 %collective-permute-start.10 = (f32[4,2,4,2,2,16,128]{6,5,4,3,2,1,0:T(8,128)S(1)}, f32[4,2,4,2,2,16,128]{6,5,4,3,2,1,0:T(8,128)S(1)}, u32[]{:S(2)}, u32[]{:S(2)}) collective-permute-start(f32[4,2,4,2,2,16,128]{6,5,4,3,2,1,0:T(8,128)S(1)} %get-tuple-element.70), channel_id=1, source_target_pairs={{0,1},{1,2},{2,3},{3,4},{4,5},{5,6},{6,7},{8,9},{9,10},{10,11},{11... | collective-permute-start | bytes 3145736 | tf_op jit(solution)/shard_map/ppermute | solution.py:545
  162.8 16.1 %collective-permute-start.11 = (f32[4,2,4,2,2,16,128]{6,5,4,3,2,1,0:T(8,128)S(1)}, f32[4,2,4,2,2,16,128]{6,5,4,3,2,1,0:T(8,128)S(1)}, u32[]{:S(2)}, u32[]{:S(2)}) collective-permute-start(f32[4,2,4,2,2,16,128]{6,5,4,3,2,1,0:T(8,128)S(1)} %get-tuple-element.71), channel_id=1, source_target_pairs={{1,0},{2,1},{3,2},{4,3},{5,4},{6,5},{7,6},{9,8},{10,9},{11,10},{12... | collective-permute-start | bytes 3145736 | tf_op jit(solution)/shard_map/ppermute | solution.py:546
  178.9 34.8 %copy-start.1 = (f32[16,12,384]{2,0,1:T(8,128)S(1)}, f32[16,12,384]{2,0,1:T(8,128)}, u32[]{:S(2)}) copy-start(f32[16,12,384]{2,0,1:T(8,128)} %param.7) | copy-start | bytes 884740

commit v3 on v2

--- a/solution.py
+++ b/solution.py
@@ -77,8 +77,9 @@
     return sums[0] + moved_x(along_x, 1 - px) + moved_z(sums[2], 1 - pz)
 
 
-def assemble_kernel(in_ref, own_ref, up_ref, down_ref):
+def assemble_kernel(in_ref, own_ref, up_ref, down_ref, done_ref):
     fields, rows = own_ref.shape[0], own_ref.shape[2]
+    done_ref[...] = jnp.zeros(done_ref.shape, jnp.float32)
 
     def one(j, carry):
         for f in range(fields):
@@ -238,11 +239,17 @@
             delta_ref[3 + d, at(j)] = damping * inverse_there[d] * (own - back)
         delta_ref[6, at(j)] = damping * change
 
-    def work(i, carry):
-        for slot in (0, 1):
-            change_row(jnp.clip(low + 2 * i - 2 + slot, low, high - 1), slot)
+    def begin(i):
         for slot in (0, 1):
             add_up(jnp.minimum(low + 2 * i + slot, high - 1), slot)
+
+    def finish(i):
+        for slot in (0, 1):
+            change_row(jnp.minimum(low + 2 * i + slot, high - 1), slot)
+
+    def work(i, carry):
+        finish(i - 1)
+        begin(i)
         return carry
 
     def apply(j, carry):
@@ -252,7 +259,10 @@
         u_ref[3, py, px, pz, at(j)] += delta_ref[6, at(j)]
         return carry
 
-    lax.fori_loop(0, (high - low + 1) // 2 + 1, work, 0)
+    pairs = (high - low + 1) // 2
+    begin(0)
+    lax.fori_loop(1, pairs, work, 0)
+    finish(pairs - 1)
     lax.fori_loop(low, high, apply, 0)
 
 
@@ -342,21 +352,37 @@
 
 def final_kernel(order_ref, old_ref, below_ref, above_ref, *refs):
     c_refs = refs[:8]
-    d_ref, f_ref, vs_ref, u_ref, out_ref, delta_ref, sums_ref, sum_ref = refs[8:]
+    d_ref, f_ref, vs_ref, u_ref, out_ref, delta_ref, sums_ref, sum_ref, apart_ref = refs[8:]
     rows = u_ref.shape[-2] // SUBLANES - 2 * Y_ROWS
     load_margins(below_ref, above_ref, u_ref, rows)
     run_sweeps(3, order_ref, u_ref, c_refs, d_ref, f_ref, delta_ref, sums_ref, rows)
-    sum_ref[...] = jnp.zeros(sum_ref.shape, jnp.float32)
+    apart_ref[...] = jnp.zeros(apart_ref.shape, jnp.float32)
 
     def residual(j, carry):
         y = j // 2
+        apart = {}
         for parity in PARITIES:
+            _, px, pz = parity
             found = partial_momentum(u_ref, c_refs, d_ref, f_ref, parity, (0, 1, 2), Y_ROWS + j)
             for d in range(3):
-                sum_ref[d, y] = sum_ref[d, y] + gathered(found[d], parity)
+                for v, slot in enumerate((0, 1 + px, 3 + pz, 5 + 2 * px + pz)):
+                    apart[d, slot] = found[d][v] + apart[d, slot] if (d, slot) in apart else found[d][v]
+        for (d, slot), value in apart.items():
+            apart_ref[d, y, slot] += value
         return carry
 
     lax.fori_loop(0, rows, residual, 0)
+    for y in range(rows // 2):
+        for d in range(3):
+            total = apart_ref[d, y, 0]
+            for px in (0, 1):
+                along_x = apart_ref[d, y, 1 + px]
+                for pz in (0, 1):
+                    along_x = along_x + moved_z(apart_ref[d, y, 5 + 2 * px + pz], 1 - pz)
+                total = total + moved_x(along_x, 1 - px)
+            for pz in (0, 1):
+                total = total + moved_z(apart_ref[d, y, 3 + pz], 1 - pz)
+            sum_ref[d, y] = total
     sublanes = SUBLANES
     cells = 2 * sublanes // 4
     weights = cycle_weights(cells)
@@ -471,24 +497,42 @@
         out_ref[(s,) + place] = found
 
 
-def pack_kernel(velocity_ref, pressure_ref, viscosity_ref, force_ref, state_ref, fixed_ref, row_ref):
-    parts = state_ref.shape[0]
-    half = state_ref.shape[5]
-    tiles = row_ref.shape[2]
-    for py in (0, 1):
-        for t in range(tiles):
-            columns = slice(LANES * t, LANES * (t + 1))
-            viscous = viscosity_ref[py, :, columns]
-            row_ref[py, 7, t] = viscous
-            row_ref[py, 3, t] = viscous * pressure_ref[py, :, columns]
-            for d in range(3):
-                row_ref[py, d, t] = velocity_ref[d, py, :, columns]
-                row_ref[py, 4 + d, t] = force_ref[d, py, :, columns]
+def write_windows(row_ref, out_ref, j):
+    parts, fields = out_ref.shape[:2]
+    half = out_ref.shape[5]
     for py in (0, 1):
         for px in (0, 1):
-            for f in range(8):
-                pieces = [row_ref[py, f, t, pl.ds(px, half, stride=2), :] for t in range(tiles)]
-                cut_windows(pieces, state_ref if f < 4 else fixed_ref, (f % 4, py, 0, px), parts)
+            for f in range(fields):
+                pieces = [row_ref[py, f, t, pl.ds(px, half, stride=2), :] for t in range(row_ref.shape[2])]
+                cut_windows(pieces, out_ref, (f, py, j, px), parts)
+
+
+def pack_fixed_kernel(force_ref, viscosity_ref, out_ref, row_ref):
+    def one(j, carry):
+        for py in (0, 1):
+            for t in range(row_ref.shape[2]):
+                columns = slice(LANES * t, LANES * (t + 1))
+                row_ref[py, 3, t] = viscosity_ref[2 * j + py, :, columns]
+                for d in range(3):
+                    row_ref[py, d, t] = force_ref[d, 2 * j + py, :, columns]
+        write_windows(row_ref, out_ref, j)
+        return carry
+
+    lax.fori_loop(0, out_ref.shape[3], one, 0)
+
+
+def pack_state_kernel(velocity_ref, viscosity_ref, pressure_ref, out_ref, row_ref):
+    def one(j, carry):
+        for py in (0, 1):
+            for t in range(row_ref.shape[2]):
+                columns = slice(LANES * t, LANES * (t + 1))
+                row_ref[py, 3, t] = viscosity_ref[2 * j + py, :, columns] * pressure_ref[2 * j + py, :, columns]
+                for d in range(3):
+                    row_ref[py, d, t] = velocity_ref[d, 2 * j + py, :, columns]
+        write_windows(row_ref, out_ref, j)
+        return carry
+
+    lax.fori_loop(0, out_ref.shape[3], one, 0)
 
 
 def unpack_kernel(back_ref, viscosity_ref, velocity_ref, pressure_ref, row_ref):
@@ -554,46 +598,50 @@
     rows = lat_cells // 2
     total = rows + 2 * Y_ROWS
     tile = (SUBLANES, LANES)
-    own = shaped(4, 2, rows, 2, 2, *tile)
     strip = shaped(4, 2, Y_ROWS, 2, 2, *tile)
-    sent = shaped(parts, 4, 2, rows, 2, lon_cells // 2, LANES)
-    sent_block = pl.BlockSpec((parts, 4, 2, 1, 2, lon_cells // 2, LANES), lambda j: (0, 0, 0, j, 0, 0, 0))
-    state_sent, fixed_sent = pl.pallas_call(
-        pack_kernel,
-        out_shape=(sent, sent),
-        grid=(rows,),
-        in_specs=[
-            pl.BlockSpec((3, 2, lon_cells, rad_cells), lambda j: (0, j, 0, 0)),
-            pl.BlockSpec((2, lon_cells, rad_cells), lambda j: (j, 0, 0)),
-            pl.BlockSpec((2, lon_cells, rad_cells), lambda j: (j, 0, 0)),
-            pl.BlockSpec((3, 2, lon_cells, rad_cells), lambda j: (0, j, 0, 0)),
-        ],
-        out_specs=(sent_block, sent_block),
-        scratch_shapes=[pltpu.VMEM((2, 8, rad_cells // LANES, lon_cells, LANES), jnp.float32)],
-        compiler_params=params(16),
-    )(*[
-        pltpu.with_memory_space_constraint(array, pltpu.HBM)
-        for array in (
-            velocity.transpose(0, 2, 1, 3), pressure_in.transpose(1, 0, 2),
-            viscosity.transpose(1, 0, 2), body_force.transpose(0, 2, 1, 3),
-        )
-    ])
+    steps = 2 - rows % 2
+    several = pl.BlockSpec((3, lat_cells // steps, lon_cells, rad_cells), lambda j: (0, j, 0, 0))
+    single = pl.BlockSpec((lat_cells // steps, lon_cells, rad_cells), lambda j: (j, 0, 0))
+
+    def packed_windows(kernel, fields, specs, *arrays):
+        return pl.pallas_call(
+            kernel,
+            out_shape=shaped(parts, fields, 2, rows, 2, lon_cells // 2, LANES),
+            grid=(steps,),
+            in_specs=specs,
+            out_specs=pl.BlockSpec(
+                (parts, fields, 2, rows // steps, 2, lon_cells // 2, LANES), lambda j: (0, 0, 0, j, 0, 0, 0)
+            ),
+            scratch_shapes=[pltpu.VMEM((2, fields, rad_cells // LANES, lon_cells, LANES), jnp.float32)],
+            compiler_params=params(12),
+        )(*[pltpu.with_memory_space_constraint(array, pltpu.HBM) for array in arrays])
 
     def assembled(pieces):
+        fields = pieces.shape[1]
+        strips = shaped(fields, 2, Y_ROWS, 2, 2, *tile)
         return pl.pallas_call(
             assemble_kernel,
-            out_shape=(own, strip, strip),
+            out_shape=(shaped(fields, 2, rows, 2, 2, *tile), strips, strips, shaped(8, LANES)),
             in_specs=[VMEM],
-            out_specs=(VMEM, VMEM, VMEM),
-            compiler_params=params(12),
+            out_specs=(VMEM, VMEM, VMEM, VMEM),
+            compiler_params=params(14),
         )(lax.all_to_all(pieces, "lon", 0, 0, tiled=True))
 
-    own_fixed, fixed_up, fixed_down = assembled(fixed_sent)
-    fixed_up, fixed_down, state_sent = lax.optimization_barrier((fixed_up, fixed_down, state_sent))
+    fixed_sent = packed_windows(
+        pack_fixed_kernel, 4, [several, single],
+        body_force.transpose(0, 2, 1, 3), viscosity.transpose(1, 0, 2),
+    )
+    state_sent = packed_windows(
+        pack_state_kernel, 4, [several, single, single],
+        velocity.transpose(0, 2, 1, 3), viscosity.transpose(1, 0, 2), pressure_in.transpose(1, 0, 2),
+    )
+    own_fixed, fixed_up, fixed_down, done = assembled(fixed_sent)
+    done, state_sent = lax.optimization_barrier((done, state_sent))
     fixed_below, fixed_above = exchange(fixed_up, fixed_down, "lat", lats)
-    own_state, state_up, state_down = assembled(state_sent)
-    below, above = exchange(state_up, state_down, "lat", lats)
+    own_state, up, down, done = assembled(state_sent)
+    below, above = exchange(up, down, "lat", lats)
     stacked = (2, 2, 2)
+    state_type = kept(4, *stacked, pitch(total), LANES)
     *couplings, diagonals, force, viscous_sum = pl.pallas_call(
         coupling_kernel,
         out_shape=(
@@ -608,7 +656,6 @@
         compiler_params=params(10),
     )(own_fixed, fixed_below, fixed_above)
     constants = [hold(array) for array in (*couplings, diagonals, force)]
-    state_type = kept(4, *stacked, pitch(total), LANES)
     scratch = [
         pltpu.VMEM((7, pitch(total), LANES), jnp.float32),
         pltpu.VMEM((2, 6, 4) + tile, jnp.float32),
@@ -656,7 +703,8 @@
         out_shape=(state_type, shaped(parts, 3, 2, rows, 2, lon_cells // 2, LANES)),
         in_specs=[SMEM] + [VMEM] * 14,
         out_specs=(VMEM, VMEM),
-        scratch_shapes=scratch + [pltpu.VMEM((3, rows // 2) + tile, jnp.float32)],
+        scratch_shapes=scratch
+        + [pltpu.VMEM((3, rows // 2) + tile, jnp.float32), pltpu.VMEM((3, rows // 2, 9) + tile, jnp.float32)],
         input_output_aliases={1: 0},
         compiler_params=params(8),
     )(colour_order, hold(state), below, above, *constants, viscous_sum)

time: 217 us -> 211 us (0.972)
  blocking collectives: 39.1 us -> 17.4 us
  waiting for transfers between devices: 66 us -> 77.4 us
  starting transfers between devices: 35.3 us -> 38.4 us
    all_to_all x1 -> x0, blocking collectives: 21.7 us -> none  [assembled(): lax.all_to_all(pieces, 'lon', 0, 0, tiled=True)]
    all_to_all x1 -> x2, waiting for transfers between devices: 11.4 us -> 24.3 us  [assembled(): lax.all_to_all(pieces, 'lon', 0, 0, tiled=True)]
    all_to_all x1 -> x2, starting transfers between devices: 3.56 us -> 7.12 us  [assembled(): lax.all_to_all(pieces, 'lon', 0, 0, tiled=True)]
    pallas_call x3 -> x4, Pallas kernels: 6.34 us -> 9.75 us  [the longest x2 6.23 us: packed_windows(): pl.pallas_call(kernel, out_shape=shaped(parts, fields, 2, rows, 2, lon_ce...]
  transfers between devices with their start and end apart: 13 -> 14, of which waited for: 11 -> 11; matrix products, arithmetic and copies ran while one was open for 0% -> 0% of each run, Pallas kernels for 5% -> 8%
where the time goes in v3:
time: 211 us
  waiting for transfers between devices  77.4 us (37%)
  Pallas kernels  74.3 us (35%)
  starting transfers between devices  38.4 us (18%)
  blocking collectives  17.4 us (8%)
  local copies, waits for them, and re-layouts  2.55 us (1%)
    ppermute x6, waiting for transfers between devices, exchange(): below = lax.ppermute(value_up, axis, [(i, i + 1) for i in range(count - 1)])  30.5 us
    all_to_all x2, waiting for transfers between devices, assembled(): lax.all_to_all(pieces, 'lon', 0, 0, tiled=True)  24.3 us
    pallas_call x2, Pallas kernels, body_windows(): pl.pallas_call(functools.partial(sweep_kernel, g), out_shape=(state_type,...  22.7 us
    ppermute x6, waiting for transfers between devices, exchange(): lax.ppermute(value_down, axis, [(i + 1, i) for i in range(count - 1)])  22.6 us
    ppermute x6, starting transfers between devices, exchange(): below = lax.ppermute(value_up, axis, [(i, i + 1) for i in range(count - 1)])  19 us
    all_to_all x1, blocking collectives, body_windows(): back = lax.all_to_all(packed, 'lon', 0, 0, tiled=True)  17.4 us
    pallas_call x1, Pallas kernels, body_windows(): pl.pallas_call(final_kernel, out_shape=(state_type, shaped(parts, 3, 2, r...  17 us
    ppermute x6, starting transfers between devices, exchange(): lax.ppermute(value_down, axis, [(i + 1, i) for i in range(count - 1)])  12.3 us
  transfers between devices with their start and end apart: 14, of which 11 were waited for; matrix products, arithmetic and copies ran while one was open for 0% of the time, Pallas kernels for 8%

profile of v3, /device:TPU:9, one launch (start us, length us, event | category | flops | bytes accessed | tf_op | source)
XLA Modules:
  0.0 210.8 jit_solution(13338568041072097355)
XLA Ops:
  0.6 3.0 %shard_map.70 = f32[4,4,2,6,2,8,128]{6,5,4,3,2,1,0:T(8,128)} custom-call(f32[3,12,16,384]{3,2,1,0:T(8,128)} %bitcast.10, f32[12,16,384]{2,1,0:T(8,128)} %bitcast.6), custom_call_target="tpu_custom_call" | custom-call | tf_op jit(solution)/shard_map/pallas_call | solution.py:607
  3.7 3.6 %all-to-all-start.1 = ((f32[4,4,2,6,2,8,128]{6,5,4,3,2,1,0:T(8,128)}), f32[4,4,2,6,2,8,128]{6,5,4,3,2,1,0:T(8,128)S(1)}, u32[]{:S(2)}, u32[]{:S(2)}) async-start(f32[4,4,2,6,2,8,128]{6,5,4,3,2,1,0:T(8,128)} %shard_map.70), calls=%async_computation.1 | async-start | bytes 3145728 | tf_op jit(solution)/shard_map/all_to_all | solution.py:628
  7.2 3.2 %shard_map.68 = f32[4,4,2,6,2,8,128]{6,5,4,3,2,1,0:T(8,128)} custom-call(f32[3,12,16,384]{3,2,1,0:T(8,128)} %bitcast.9, f32[12,16,384]{2,1,0:T(8,128)} %bitcast.7, f32[12,16,384]{2,1,0:T(8,128)} %bitcast.11), custom_call_target="tpu_custom_call" | custom-call | tf_op jit(solution)/shard_map/pallas_call | solution.py:607
  10.4 15.5 %all-to-all-done.1.in_ref = f32[4,4,2,6,2,8,128]{6,5,4,3,2,1,0:T(8,128)S(1)} async-done(((f32[4,4,2,6,2,8,128]{6,5,4,3,2,1,0:T(8,128)}), f32[4,4,2,6,2,8,128]{6,5,4,3,2,1,0:T(8,128)S(1)}, u32[]{:S(2)}, u32[]{:S(2)}) %all-to-all-start.1) | async-done | bytes 1572896 | tf_op jit(solution)/shard_map/all_to_all | solution.py:628
  25.9 3.6 %all-to-all-start = ((f32[4,4,2,6,2,8,128]{6,5,4,3,2,1,0:T(8,128)}), f32[4,4,2,6,2,8,128]{6,5,4,3,2,1,0:T(8,128)S(1)}, u32[]{:S(2)}, u32[]{:S(2)}) async-start(f32[4,4,2,6,2,8,128]{6,5,4,3,2,1,0:T(8,128)} %shard_map.68), calls=%async_computation | async-start | bytes 3145728 | tf_op jit(solution)/shard_map/all_to_all | solution.py:628
  32.9 4.6 %collective-permute-start.2 = (f32[4,2,4,2,2,16,128]{6,5,4,3,2,1,0:T(8,128)}, f32[4,2,4,2,2,16,128]{6,5,4,3,2,1,0:T(8,128)S(1)}, u32[]{:S(2)}, u32[]{:S(2)}) collective-permute-start(f32[4,2,4,2,2,16,128]{6,5,4,3,2,1,0:T(8,128)} %get-tuple-element.38), channel_id=1, source_target_pairs={{0,1},{1,2},{2,3},{3,4},{4,5},{5,6},{6,7},{8,9},{9,10},{10,11},{11... | collective-permute-start | bytes 3145736 | tf_op jit(solution)/shard_map/ppermute | solution.py:589
  39.4 8.8 %all-to-all-done.in_ref = f32[4,4,2,6,2,8,128]{6,5,4,3,2,1,0:T(8,128)S(1)} async-done(((f32[4,4,2,6,2,8,128]{6,5,4,3,2,1,0:T(8,128)}), f32[4,4,2,6,2,8,128]{6,5,4,3,2,1,0:T(8,128)S(1)}, u32[]{:S(2)}, u32[]{:S(2)}) %all-to-all-start) | async-done | bytes 1572896 | tf_op jit(solution)/shard_map/all_to_all | solution.py:628
  49.4 4.6 %collective-permute-start = (f32[4,2,4,2,2,16,128]{6,5,4,3,2,1,0:T(8,128)S(1)}, f32[4,2,4,2,2,16,128]{6,5,4,3,2,1,0:T(8,128)S(1)}, u32[]{:S(2)}, u32[]{:S(2)}) collective-permute-start(f32[4,2,4,2,2,16,128]{6,5,4,3,2,1,0:T(8,128)S(1)} %get-tuple-element.35), channel_id=1, source_target_pairs={{0,1},{1,2},{2,3},{3,4},{4,5},{5,6},{6,7},{8,9},{9,10},{10,11},{11... | collective-permute-start | bytes 3145736 | tf_op jit(solution)/shard_map/ppermute | solution.py:589
  57.4 9.2 %shard_map.72 = (f32[26,232,128]{2,1,0:T(8,128)S(1)}, f32[26,232,128]{2,1,0:T(8,128)S(1)}, f32[26,232,128]{2,1,0:T(8,128)S(1)}, f32[26,232,128]{2,1,0:T(8,128)S(...) custom-call(f32[4,2,6,2,2,16,128]{6,5,4,3,2,1,0:T(8,128)S(1)} %copy-, ...), custom_call_target="tpu_custom_call" | custom-call | tf_op jit(solution)/shard_map/pallas_call | solution.py:645
  66.6 3.5 %collective-permute-done.1.above_ref = f32[4,2,4,2,2,16,128]{6,5,4,3,2,1,0:T(8,128)S(1)} collective-permute-done((f32[4,2,4,2,2,16,128]{6,5,4,3,2,1,0:T(8,128)S(1)}, f32[4,2,4,2,2,16,128]{6,5,4,3,2,1,0:T(8,128)S(1)}, u32[]{:S(2)}, u32[]{:S(2)}) %collective-permute-start.1) | collective-permute-done | bytes 1048608 | tf_op jit(solution)/shard_map/ppermute | solution.py:590
  70.2 10.3 %shard_map.73 = (f32[4,2,2,2,232,128]{5,4,3,2,1,0:T(8,128)S(1)}, f32[4,2,4,2,2,16,128]{6,5,4,3,2,1,0:T(8,128)S(1)}, f32[4,2,4,2,2,16,128]{6,5,4,3,2,1,0:T(8,128)S(1)}) custom-call(s32[8]{0:T(128)S(1)} %copy-done.3, f32[4,2,6,2,2,16,128]{6,5,4,3,2,1,0:T(8,128)S(1)} %get-tuple-element.34.own_ref, ...), custom_call_target="tpu_custom_call" | custom-call | tf_op jit(solution)/shard_map/pallas_call | solution.py:663
  85.0 9.1 %collective-permute-done.4.below_ref = f32[4,2,4,2,2,16,128]{6,5,4,3,2,1,0:T(8,128)S(1)} collective-permute-done((f32[4,2,4,2,2,16,128]{6,5,4,3,2,1,0:T(8,128)S(1)}, f32[4,2,4,2,2,16,128]{6,5,4,3,2,1,0:T(8,128)S(1)}, u32[]{:S(2)}, u32[]{:S(2)}) %collective-permute-start.4) | collective-permute-done | bytes 1048608 | tf_op jit(solution)/shard_map/ppermute | solution.py:589
  94.1 4.4 %collective-permute-done.5.above_ref = f32[4,2,4,2,2,16,128]{6,5,4,3,2,1,0:T(8,128)S(1)} collective-permute-done((f32[4,2,4,2,2,16,128]{6,5,4,3,2,1,0:T(8,128)S(1)}, f32[4,2,4,2,2,16,128]{6,5,4,3,2,1,0:T(8,128)S(1)}, u32[]{:S(2)}, u32[]{:S(2)}) %collective-permute-start.5) | collective-permute-done | bytes 1048608 | tf_op jit(solution)/shard_map/ppermute | solution.py:590
  98.5 12.5 %shard_map.74 = (f32[4,2,2,2,232,128]{5,4,3,2,1,0:T(8,128)S(1)}, f32[4,2,4,2,2,16,128]{6,5,4,3,2,1,0:T(8,128)}, f32[4,2,4,2,2,16,128]{6,5,4,3,2,1,0:T(8,128)}) custom-call(s32[8]{0:T(128)S(1)} %copy-done.3, f32[4,2,2,2,232,128]{5,4,3,2,1,0:T(8,128)S(1)} %get-tuple-element.50.old_ref, ...), custom_call_target="tpu_custom_call", output_to_operand_aliasing={{0}: (1, {})} | custom-call | tf_op jit(solution)/shard_map/pallas_call | solution.py:673
  112.2 3.1 %collective-permute-start.6 = (f32[2,6,2,16,128]{4,3,2,1,0:T(8,128)S(1)}, f32[2,6,2,16,128]{4,3,2,1,0:T(8,128)S(1)}, u32[]{:S(2)}, u32[]{:S(2)}) collective-permute-start(f32[2,6,2,16,128]{4,3,2,1,0:T(8,128)S(1)} %get-tuple-element.54), channel_id=1, source_target_pairs={{0,8},{8,16},{16,24},{1,9},{9,17},{17,25},{2,10},{10,18},{18,26},{... | collective-permute-start | bytes 589832 | tf_op jit(solution)/shard_map/ppermute | solution.py:589
  119.0 5.9 %collective-permute-done.7.from_right_ref = f32[2,6,2,16,128]{4,3,2,1,0:T(8,128)S(1)} collective-permute-done((f32[2,6,2,16,128]{4,3,2,1,0:T(8,128)S(1)}, f32[2,6,2,16,128]{4,3,2,1,0:T(8,128)S(1)}, u32[]{:S(2)}, u32[]{:S(2)}) %collective-permute-start.7) | collective-permute-done | bytes 196640 | tf_op jit(solution)/shard_map/ppermute | solution.py:590
  131.0 9.8 %collective-permute-done.8.below_ref = f32[4,2,4,2,2,16,128]{6,5,4,3,2,1,0:T(8,128)S(1)} collective-permute-done((f32[4,2,4,2,2,16,128]{6,5,4,3,2,1,0:T(8,128)S(1)}, f32[4,2,4,2,2,16,128]{6,5,4,3,2,1,0:T(8,128)S(1)}, u32[]{:S(2)}, u32[]{:S(2)}) %collective-permute-start.8) | collective-permute-done | bytes 1048608 | tf_op jit(solution)/shard_map/ppermute | solution.py:589
  140.8 4.4 %collective-permute-done.9.above_ref = f32[4,2,4,2,2,16,128]{6,5,4,3,2,1,0:T(8,128)S(1)} collective-permute-done((f32[4,2,4,2,2,16,128]{6,5,4,3,2,1,0:T(8,128)S(1)}, f32[4,2,4,2,2,16,128]{6,5,4,3,2,1,0:T(8,128)S(1)}, u32[]{:S(2)}, u32[]{:S(2)}) %collective-permute-start.9) | collective-permute-done | bytes 1048608 | tf_op jit(solution)/shard_map/ppermute | solution.py:590
  145.2 10.2 %shard_map.77 = (f32[4,2,2,2,232,128]{5,4,3,2,1,0:T(8,128)S(1)}, f32[4,2,4,2,2,16,128]{6,5,4,3,2,1,0:T(8,128)S(1)}, f32[4,2,4,2,2,16,128]{6,5,4,3,2,1,0:T(8,128)S(1)}) custom-call(s32[8]{0:T(128)S(1)} %copy-done.3, f32[4,2,2,2,232,128]{5,4,3,2,1,0:T(8,128)S(1)} %get-tuple-element.56.old_ref, ...), custom_call_target="tpu_custom_call", output_to_operand_aliasing={{0}: (1, {})} | custom-call | tf_op jit(solution)/shard_map/pallas_call | solution.py:673
  160.0 9.1 %collective-permute-done.10.below_ref = f32[4,2,4,2,2,16,128]{6,5,4,3,2,1,0:T(8,128)S(1)} collective-permute-done((f32[4,2,4,2,2,16,128]{6,5,4,3,2,1,0:T(8,128)S(1)}, f32[4,2,4,2,2,16,128]{6,5,4,3,2,1,0:T(8,128)S(1)}, u32[]{:S(2)}, u32[]{:S(2)}) %collective-permute-start.10) | collective-permute-done | bytes 1048608 | tf_op jit(solution)/shard_map/ppermute | solution.py:589
  169.1 4.4 %collective-permute-done.11.above_ref = f32[4,2,4,2,2,16,128]{6,5,4,3,2,1,0:T(8,128)S(1)} collective-permute-done((f32[4,2,4,2,2,16,128]{6,5,4,3,2,1,0:T(8,128)S(1)}, f32[4,2,4,2,2,16,128]{6,5,4,3,2,1,0:T(8,128)S(1)}, u32[]{:S(2)}, u32[]{:S(2)}) %collective-permute-start.11) | collective-permute-done | bytes 1048608 | tf_op jit(solution)/shard_map/ppermute | solution.py:590
  173.5 17.0 %shard_map.78 = (f32[4,2,2,2,232,128]{5,4,3,2,1,0:T(8,128)S(1)}, f32[4,3,2,6,2,8,128]{6,5,4,3,2,1,0:T(8,128)S(1)}) custom-call(s32[8]{0:T(128)S(1)} %copy-done.3, f32[4,2,2,2,232,128]{5,4,3,2,1,0:T(8,128)S(1)} %get-tuple-element.59.old_ref, f32[4,2,4,2,2,16,128]{6,5,4,3,2,1,0:T(8,128)S(1)} %collective-permute-done.10.below_ref, ...), custom_call_target="tpu_custom_call", output_to_operand_aliasing={{0}: (1, {})} | custom-call | tf_op jit(solution)/shard_map/pallas_call | solution.py:701
  190.5 17.4 %all_to_all.15.back_ref = f32[4,3,2,6,2,8,128]{6,5,4,3,2,1,0:T(8,128)S(1)} all-to-all(f32[4,3,2,6,2,8,128]{6,5,4,3,2,1,0:T(8,128)S(1)} %get-tuple-element.63), channel_id=1, replica_groups=mesh['lon'=4,'lat'=8] {'lon'}, dimensions={0} | all-to-all | bytes 2359296 | tf_op jit(solution)/shard_map/all_to_all | solution.py:711
  207.8 2.9 %shard_map.79 = (f32[3,12,16,384]{3,2,1,0:T(8,128)}, f32[12,16,384]{2,1,0:T(8,128)}) custom-call(f32[4,3,2,6,2,8,128]{6,5,4,3,2,1,0:T(8,128)S(1)} %all_to_all.15.back_ref, f32[12,16,384]{2,1,0:T(8,128)S(1)} %bitcast.8), custom_call_target="tpu_custom_call" | custom-call | tf_op jit(solution)/shard_map/pallas_call | solution.py:712
  (25 shorter events, 30.0 us)
Async XLA Ops:
  3.7 22.3 %all-to-all-start.1 = ((f32[4,4,2,6,2,8,128]{6,5,4,3,2,1,0:T(8,128)}), f32[4,4,2,6,2,8,128]{6,5,4,3,2,1,0:T(8,128)S(1)}, u32[]{:S(2)}, u32[]{:S(2)}) async-start(f32[4,4,2,6,2,8,128]{6,5,4,3,2,1,0:T(8,128)} %shard_map.70), calls=%async_computation.1 | async-start | bytes 3145728 | tf_op jit(solution)/shard_map/all_to_all | solution.py:628
  25.9 22.2 %all-to-all-start = ((f32[4,4,2,6,2,8,128]{6,5,4,3,2,1,0:T(8,128)}), f32[4,4,2,6,2,8,128]{6,5,4,3,2,1,0:T(8,128)S(1)}, u32[]{:S(2)}, u32[]{:S(2)}) async-start(f32[4,4,2,6,2,8,128]{6,5,4,3,2,1,0:T(8,128)} %shard_map.68), calls=%async_computation | async-start | bytes 3145728 | tf_op jit(solution)/shard_map/all_to_all | solution.py:628
  29.5 40.7 %copy-start.3 = (s32[8]{0:T(128)S(1)}, s32[8]{0:T(128)}, u32[]{:S(2)}) copy-start(s32[8]{0:T(128)} %order_ref.7) | copy-start | bytes 100
  31.8 1.1 copy-start.1
  32.9 23.1 %collective-permute-start.2 = (f32[4,2,4,2,2,16,128]{6,5,4,3,2,1,0:T(8,128)}, f32[4,2,4,2,2,16,128]{6,5,4,3,2,1,0:T(8,128)S(1)}, u32[]{:S(2)}, u32[]{:S(2)}) collective-permute-start(f32[4,2,4,2,2,16,128]{6,5,4,3,2,1,0:T(8,128)} %get-tuple-element.38), channel_id=1, source_target_pairs={{0,1},{1,2},{2,3},{3,4},{4,5},{5,6},{6,7},{8,9},{9,10},{10,11},{11... | collective-permute-start | bytes 3145736 | tf_op jit(solution)/shard_map/ppermute | solution.py:589
  37.5 18.5 %collective-permute-start.3 = (f32[4,2,4,2,2,16,128]{6,5,4,3,2,1,0:T(8,128)}, f32[4,2,4,2,2,16,128]{6,5,4,3,2,1,0:T(8,128)}, u32[]{:S(2)}, u32[]{:S(2)}) collective-permute-start(f32[4,2,4,2,2,16,128]{6,5,4,3,2,1,0:T(8,128)} %get-tuple-element.39), channel_id=1, source_target_pairs={{1,0},{2,1},{3,2},{4,3},{5,4},{6,5},{7,6},{9,8},{10,9},{11,10},{12... | collective-permute-start | bytes 3145736 | tf_op jit(solution)/shard_map/ppermute | solution.py:590
  49.4 17.2 %collective-permute-start = (f32[4,2,4,2,2,16,128]{6,5,4,3,2,1,0:T(8,128)S(1)}, f32[4,2,4,2,2,16,128]{6,5,4,3,2,1,0:T(8,128)S(1)}, u32[]{:S(2)}, u32[]{:S(2)}) collective-permute-start(f32[4,2,4,2,2,16,128]{6,5,4,3,2,1,0:T(8,128)S(1)} %get-tuple-element.35), channel_id=1, source_target_pairs={{0,1},{1,2},{2,3},{3,4},{4,5},{5,6},{6,7},{8,9},{9,10},{10,11},{11... | collective-permute-start | bytes 3145736 | tf_op jit(solution)/shard_map/ppermute | solution.py:589
  54.0 16.1 %collective-permute-start.1 = (f32[4,2,4,2,2,16,128]{6,5,4,3,2,1,0:T(8,128)S(1)}, f32[4,2,4,2,2,16,128]{6,5,4,3,2,1,0:T(8,128)S(1)}, u32[]{:S(2)}, u32[]{:S(2)}) collective-permute-start(f32[4,2,4,2,2,16,128]{6,5,4,3,2,1,0:T(8,128)S(1)} %get-tuple-element.36), channel_id=1, source_target_pairs={{1,0},{2,1},{3,2},{4,3},{5,4},{6,5},{7,6},{9,8},{10,9},{11,10},{12... | collective-permute-start | bytes 3145736 | tf_op jit(solution)/shard_map/ppermute | solution.py:590
  56.0 1.4 copy-start.2
  80.5 13.7 %collective-permute-start.4 = (f32[4,2,4,2,2,16,128]{6,5,4,3,2,1,0:T(8,128)S(1)}, f32[4,2,4,2,2,16,128]{6,5,4,3,2,1,0:T(8,128)S(1)}, u32[]{:S(2)}, u32[]{:S(2)}) collective-permute-start(f32[4,2,4,2,2,16,128]{6,5,4,3,2,1,0:T(8,128)S(1)} %get-tuple-element.51), channel_id=1, source_target_pairs={{0,1},{1,2},{2,3},{3,4},{4,5},{5,6},{6,7},{8,9},{9,10},{10,11},{11... | collective-permute-start | bytes 3145736 | tf_op jit(solution)/shard_map/ppermute | solution.py:589
  82.4 16.1 %collective-permute-start.5 = (f32[4,2,4,2,2,16,128]{6,5,4,3,2,1,0:T(8,128)S(1)}, f32[4,2,4,2,2,16,128]{6,5,4,3,2,1,0:T(8,128)S(1)}, u32[]{:S(2)}, u32[]{:S(2)}) collective-permute-start(f32[4,2,4,2,2,16,128]{6,5,4,3,2,1,0:T(8,128)S(1)} %get-tuple-element.52), channel_id=1, source_target_pairs={{1,0},{2,1},{3,2},{4,3},{5,4},{6,5},{7,6},{9,8},{10,9},{11,10},{12... | collective-permute-start | bytes 3145736 | tf_op jit(solution)/shard_map/ppermute | solution.py:590
  112.2 6.9 %collective-permute-start.6 = (f32[2,6,2,16,128]{4,3,2,1,0:T(8,128)S(1)}, f32[2,6,2,16,128]{4,3,2,1,0:T(8,128)S(1)}, u32[]{:S(2)}, u32[]{:S(2)}) collective-permute-start(f32[2,6,2,16,128]{4,3,2,1,0:T(8,128)S(1)} %get-tuple-element.54), channel_id=1, source_target_pairs={{0,8},{8,16},{16,24},{1,9},{9,17},{17,25},{2,10},{10,18},{18,26},{... | collective-permute-start | bytes 589832 | tf_op jit(solution)/shard_map/ppermute | solution.py:589
  115.2 9.7 %collective-permute-start.7 = (f32[2,6,2,16,128]{4,3,2,1,0:T(8,128)S(1)}, f32[2,6,2,16,128]{4,3,2,1,0:T(8,128)S(1)}, u32[]{:S(2)}, u32[]{:S(2)}) collective-permute-start(f32[2,6,2,16,128]{4,3,2,1,0:T(8,128)S(1)} %get-tuple-element.55), channel_id=1, source_target_pairs={{8,0},{16,8},{24,16},{9,1},{17,9},{25,17},{10,2},{18,10},{26,18},{... | collective-permute-start | bytes 589832 | tf_op jit(solution)/shard_map/ppermute | solution.py:590
  126.2 14.6 %collective-permute-start.8 = (f32[4,2,4,2,2,16,128]{6,5,4,3,2,1,0:T(8,128)S(1)}, f32[4,2,4,2,2,16,128]{6,5,4,3,2,1,0:T(8,128)S(1)}, u32[]{:S(2)}, u32[]{:S(2)}) collective-permute-start(f32[4,2,4,2,2,16,128]{6,5,4,3,2,1,0:T(8,128)S(1)} %get-tuple-element.57), channel_id=1, source_target_pairs={{0,1},{1,2},{2,3},{3,4},{4,5},{5,6},{6,7},{8,9},{9,10},{10,11},{11... | collective-permute-start | bytes 3145736 | tf_op jit(solution)/shard_map/ppermute | solution.py:589
  129.1 16.1 %collective-permute-start.9 = (f32[4,2,4,2,2,16,128]{6,5,4,3,2,1,0:T(8,128)S(1)}, f32[4,2,4,2,2,16,128]{6,5,4,3,2,1,0:T(8,128)S(1)}, u32[]{:S(2)}, u32[]{:S(2)}) collective-permute-start(f32[4,2,4,2,2,16,128]{6,5,4,3,2,1,0:T(8,128)S(1)} %get-tuple-element.58), channel_id=1, source_target_pairs={{1,0},{2,1},{3,2},{4,3},{5,4},{6,5},{7,6},{9,8},{10,9},{11,10},{12... | collective-permute-start | bytes 3145736 | tf_op jit(solution)/shard_map/ppermute | solution.py:590
  155.4 13.7 %collective-permute-start.10 = (f32[4,2,4,2,2,16,128]{6,5,4,3,2,1,0:T(8,128)S(1)}, f32[4,2,4,2,2,16,128]{6,5,4,3,2,1,0:T(8,128)S(1)}, u32[]{:S(2)}, u32[]{:S(2)}) collective-permute-start(f32[4,2,4,2,2,16,128]{6,5,4,3,2,1,0:T(8,128)S(1)} %get-tuple-element.60), channel_id=1, source_target_pairs={{0,1},{1,2},{2,3},{3,4},{4,5},{5,6},{6,7},{8,9},{9,10},{10,11},{11... | collective-permute-start | bytes 3145736 | tf_op jit(solution)/shard_map/ppermute | solution.py:589
  157.4 16.1 %collective-permute-start.11 = (f32[4,2,4,2,2,16,128]{6,5,4,3,2,1,0:T(8,128)S(1)}, f32[4,2,4,2,2,16,128]{6,5,4,3,2,1,0:T(8,128)S(1)}, u32[]{:S(2)}, u32[]{:S(2)}) collective-permute-start(f32[4,2,4,2,2,16,128]{6,5,4,3,2,1,0:T(8,128)S(1)} %get-tuple-element.61), channel_id=1, source_target_pairs={{1,0},{2,1},{3,2},{4,3},{5,4},{6,5},{7,6},{9,8},{10,9},{11,10},{12... | collective-permute-start | bytes 3145736 | tf_op jit(solution)/shard_map/ppermute | solution.py:590
  173.5 34.3 %copy-start = (f32[16,12,384]{2,0,1:T(8,128)S(1)}, f32[16,12,384]{2,0,1:T(8,128)}, u32[]{:S(2)}) copy-start(f32[16,12,384]{2,0,1:T(8,128)} %param.7) | copy-start | bytes 884740
